TPU v7x, 256 devices: a whole 4x4x8 slice. The times are simulated.
256 devices in a mesh: gx: 16 (over z_lo, y, core), gy: 4 (over z_hi), gz: 4 (over x).
Axes of the slice: x: 4, y: 4, z: 8 (z_hi: 4, z_lo: 2; z = z_hi * 2 + z_lo), core: 2. Of those that a mesh axis runs over, the one named last changes fastest.
Arguments:
- positions: float32 [16, 4, 128, 3, 2, 128], P('gx', 'gy', 'gz'), may hold values from 0 to 1
- velocities: float32 [16, 4, 128, 3, 2, 128], P('gx', 'gy', 'gz'), may hold values from -6 to 6
- strength: float32 [16, 4, 128, 2, 128], P('gx', 'gy', 'gz'), may hold values from 0.05 to 0.4
- cluster_count: int32 [16, 4, 128], P('gx', 'gy', 'gz'), may hold values from 1 to 2, as said below
- migrant_ids: int32 [16, 4, 128, 1], P('gx', 'gy', 'gz'), may hold values from 0 to 1
- destination: int32 [16, 4, 128], replicated, may hold values from 0 to 5
- pair_i: int32 [16, 4, 128, 16], P('gx', 'gy', 'gz'), may hold values from 0 to 7
- pair_j: int32 [16, 4, 128, 16], P('gx', 'gy', 'gz'), may hold values from 0 to 111
- pair_count: int32 [16, 4, 128], P('gx', 'gy', 'gz'), may hold values from 4 to 16, as said below
Outputs:
- moved: float32 [16, 4, 128, 6, 8, 128], P('gx', 'gy', 'gz')
- forces: float32 [16, 4, 128, 3, 8, 128], P('gx', 'gy', 'gz')
Inputs may be any that keep to these rules, and one draw needn't show every extreme that they name: `cluster_count`: some cell has all 2 slots occupied. `pair_count`: some cell has all 16 slots live.
All inputs are finite; a program needn't handle non-finite values.
Results may differ from a plain program's by a relative error of at most 0.0003.
Values sent between devices are 32-bit elements; how exact they have to be, the bound alone decides.
No kernel may reach another device: no remote copies, remote signals or barrier semaphores. Data moves between devices by JAX's collectives and lax.ppermute only.
A program may use at most 64 MiB of HBM per device.

v0:
```python
import math

import jax
import jax.numpy as jnp
from jax import lax
from jax.sharding import PartitionSpec as P

FACES = ((-1, 0, 0), (1, 0, 0), (0, -1, 0), (0, 1, 0), (0, 0, -1), (0, 0, 1))
SHELL = (
    (0, 0, 0),
    (0, 0, 1),
    (0, 1, -1),
    (0, 1, 0),
    (0, 1, 1),
    (1, -1, -1),
    (1, -1, 0),
    (1, -1, 1),
    (1, 0, -1),
    (1, 0, 0),
    (1, 0, 1),
    (1, 1, -1),
    (1, 1, 0),
    (1, 1, 1),
)
STEP = 0.01
SOFTEN = 0.1
block_pairs = 32
exact = lax.Precision.HIGHEST


def extended_2(array, sides, width):
    for axis, dim in sides:
        size, length = (lax.axis_size(axis), array.shape[dim])
        up = [(i, (i + 1) % size) for i in range(size)]
        down = [(j, i) for i, j in up]
        last = lax.slice_in_dim(array, length - width, length, axis=dim)
        initial = lax.slice_in_dim(array, 0, width, axis=dim)
        before = lax.ppermute(last, axis, up)
        after = lax.ppermute(initial, axis, down)
        array = jnp.concatenate([before, array, after], axis=dim)
    return array


def from_behind(array, axis, by):
    size = lax.axis_size(axis)
    return lax.ppermute(array, axis, [(i, (i + by) % size) for i in range(size)])


def shifted(block, offset):
    rows = block.shape[1]
    vector = jnp.array(
        [float(offset[0]), float(offset[1]), float(offset[2])] + [0.0] * (rows - 3),
        dtype=jnp.float32,
    )
    return block + vector.reshape((1, rows, 1, 1))


def collect(framed, cells):
    inner = framed[0, 2 : 2 + cells] + framed[2, 2 : 2 + cells] + framed[4, 2 : 2 + cells]
    lowest = framed[0, 0] + framed[2, 0] + framed[4, 0]
    highest = framed[0, cells + 3] + framed[2, cells + 3] + framed[4, cells + 3]
    inner = inner.at[0].add(lowest)
    return inner.at[cells - 1].add(highest)


def tile_group(coords_block, partner_block, first, second, alive):
    ext_count = coords_block.shape[2]
    partner_count = partner_block.shape[2]
    atom_count = coords_block.shape[3]
    hot_first = (first[:, :, None] == jnp.arange(ext_count, dtype=jnp.int32)[None, None, :]).astype(
        jnp.float32
    )
    hot_second = (
        second[:, :, None] == jnp.arange(partner_count, dtype=jnp.int32)[None, None, :]
    ).astype(jnp.float32)
    left = jnp.einsum("cge,cxea->cgxa", hot_first, coords_block, precision=exact)
    right = jnp.einsum("cgp,cxpa->cgxa", hot_second, partner_block, precision=exact)
    diff = left[:, :, 0:3, :, None] - right[:, :, 0:3, None, :]
    dist = jnp.sum(diff * diff, axis=2)
    reach = jnp.maximum(1.0 - dist, 0.0)
    lower = (
        jnp.arange(atom_count, dtype=jnp.int32)[:, None]
        < jnp.arange(atom_count, dtype=jnp.int32)[None, :]
    )
    same = (first == second)[:, :, None, None]
    allowed = alive[:, :, None, None] & (jnp.logical_not(same) | lower[None, None])
    weight = jnp.where(
        allowed,
        left[:, :, 3, :, None] * right[:, :, 3, None, :] * reach * reach / (dist + SOFTEN),
        0.0,
    )
    push = weight[:, :, None] * diff
    on_left = jnp.sum(push, axis=4)
    on_right = -jnp.sum(push, axis=3)
    own = jnp.einsum("cge,cgxa->cxea", hot_first, on_left, precision=exact)
    other = jnp.einsum("cgp,cgxa->cxpa", hot_second, on_right, precision=exact)
    return (own, other)


def per_device(
    positions,
    velocities,
    strength,
    cluster_count,
    migrant_ids,
    destination,
    pair_i,
    pair_j,
    pair_count,
):
    state = jnp.concatenate([positions[0, 0], velocities[0, 0], strength[0, 0][:, None]], axis=1)
    cells, _, slot_count, atom_count = state.shape
    slots = jnp.arange(slot_count, dtype=jnp.int32)
    ids = migrant_ids[0, 0]
    counts = cluster_count[0, 0]
    leaving = jnp.any(slots[None, :, None] == ids[:, None, :], axis=2)
    keep = ((slots[None, :] < counts[:, None]) & jnp.logical_not(leaving)).astype(jnp.float32)
    staying = state * keep[:, None, :, None]
    index = jnp.broadcast_to(ids[:, None, :, None], (cells, 7, ids.shape[1], atom_count))
    filled = (ids < counts[:, None]).astype(jnp.float32)
    outgoing = jnp.take_along_axis(state, index, axis=2) * filled[:, None, :, None]
    arrived = extended_2(outgoing[None, None], (("gx", 0), ("gy", 1), ("gz", 2)), 1)
    place_x = lax.axis_index("gx")
    place_y = lax.axis_index("gy")
    place_z = lax.axis_index("gz")
    extent = destination.shape
    zcells = place_z * cells + jnp.arange(cells, dtype=jnp.int32)
    inbox = []
    for face in range(6):
        offset = FACES[face]
        piece = arrived[1 + offset[0], 1 + offset[1], 1 + offset[2] : 1 + offset[2] + cells]
        line = destination[(place_x + offset[0]) % extent[0], (place_y + offset[1]) % extent[1]]
        heading = jnp.take(line, (zcells + offset[2]) % extent[2])
        valid = (heading == face).astype(jnp.float32)
        inbox.append(shifted(piece, offset) * valid[:, None, None, None])
    extended = jnp.concatenate([staying] + inbox, axis=2)
    coords = jnp.concatenate([extended[:, 0:3], extended[:, 6:7]], axis=1)
    ext_count = coords.shape[2]
    near = extended_2(coords[None], (("gy", 0), ("gz", 1)), 1)
    far = from_behind(near, "gx", -1)
    layers = (near, far)
    partners = jnp.concatenate(
        [
            shifted(layers[offset[0]][1 + offset[1], 1 + offset[2] : 1 + offset[2] + cells], offset)
            for offset in SHELL
        ],
        axis=2,
    )
    partner_count = partners.shape[2]
    list_len = pair_i.shape[3]
    first_all = pair_i[0, 0]
    second_all = pair_j[0, 0]
    live_all = pair_count[0, 0]
    alive_all = jnp.arange(list_len, dtype=jnp.int32)[None, :] < live_all[:, None]
    per_turn = math.gcd(cells, max(1, block_pairs // list_len))
    turns = cells // per_turn

    def scan_step(carry, inputs):
        coords_block, partner_block, first, second, alive = inputs
        return (carry, tile_group(coords_block, partner_block, first, second, alive))

    blocks = (
        coords.reshape((turns, per_turn) + coords.shape[1:]),
        partners.reshape((turns, per_turn) + partners.shape[1:]),
        first_all.reshape((turns, per_turn, list_len)),
        second_all.reshape((turns, per_turn, list_len)),
        alive_all.reshape((turns, per_turn, list_len)),
    )
    _, results = lax.scan(scan_step, 0, blocks)
    own_force = results[0].reshape((cells, 3, ext_count, atom_count))
    partner_force = results[1].reshape((cells, 3, partner_count, atom_count))
    partner_force = partner_force.reshape((cells, 3, 14, ext_count, atom_count))
    near_grid = jnp.zeros((3, cells + 2, 3, ext_count, atom_count), jnp.float32)
    far_grid = jnp.zeros((3, cells + 2, 3, ext_count, atom_count), jnp.float32)
    for block in range(1, 14):
        offset = SHELL[block]
        piece = partner_force[:, :, block]
        if offset[0] == 0:
            near_grid = near_grid.at[1 + offset[1], 1 + offset[2] : 1 + offset[2] + cells].add(
                piece
            )
        else:
            far_grid = far_grid.at[1 + offset[1], 1 + offset[2] : 1 + offset[2] + cells].add(piece)
    behind = from_behind(far_grid, "gx", 1)
    framed = extended_2(near_grid + behind, (("gy", 0), ("gz", 1)), 1)
    arriving = collect(framed, cells)
    forces = own_force + partner_force[:, :, 0] + arriving
    new_velocity = extended[:, 3:6] + STEP * forces
    new_position = extended[:, 0:3] + STEP * new_velocity
    moved = jnp.concatenate([new_position, new_velocity], axis=1)
    return (moved[None, None], forces[None, None])


def solution(mesh):
    in_specs = (
        P("gx", "gy", "gz", None, None, None),
        P("gx", "gy", "gz", None, None, None),
        P("gx", "gy", "gz", None, None),
        P("gx", "gy", "gz"),
        P("gx", "gy", "gz", None),
        P(),
        P("gx", "gy", "gz", None),
        P("gx", "gy", "gz", None),
        P("gx", "gy", "gz"),
    )
    out_specs = (P("gx", "gy", "gz", None, None, None), P("gx", "gy", "gz", None, None, None))
    return jax.shard_map(
        per_device, mesh=mesh, in_specs=in_specs, out_specs=out_specs, check_vma=False
    )
```

profile of v0, /device:TPU:70, one launch (start us, length us, event | category | flops | bytes accessed | tf_op | source)
XLA Modules:
  0.0 636.9 jit_solution(9429853187796623579)
XLA Ops:
  5.0 290.1 %gather_fusion = f32[28672]{0:T(1024)S(1)} fusion(f32[32,7,2,128]{3,2,1,0:T(2,128)S(1)} %get-tuple-element.253, s32[28672]{0:T(1024)S(1)} %reshape.1157), kind=kCustom, calls=%fused_computation.6 | custom fusion | bytes 688128 | tf_op jit(solution)/shard_map/jit(take_along_axis)/gather | solution.py:121
  305.0 4.5 collective-permute-start.2
  309.8 13.0 %collective-permute-done.3 = f32[3,1,32,7,1,128]{5,4,3,2,1,0:T(1,128)S(1)} collective-permute-done((f32[3,1,32,7,1,128]{5,4,3,2,1,0:T(1,128)S(1)}, f32[3,1,32,7,1,128]{5,4,3,2,1,0:T(1,128)S(1)}, u32[]{:S(2)}, u32[]{:S(2)}) %collective-permute-start.3) | collective-permute-done | bytes 344096 | tf_op jit(solution)/shard_map/ppermute | solution.py:39
  336.8 18.1 %collective-permute-done.6 = f32[1,32,4,8,128]{4,3,2,1,0:T(8,128)S(1)} collective-permute-done((f32[1,32,4,8,128]{4,3,2,1,0:T(8,128)S(1)}, f32[1,32,4,8,128]{4,3,2,1,0:T(8,128)S(1)}, u32[]{:S(2)}, u32[]{:S(2)}) %collective-permute-start.6) | collective-permute-done | bytes 524320 | tf_op jit(solution)/shard_map/ppermute | solution.py:38
  373.4 14.4 %collective-permute-done.10 = f32[3,34,4,8,128]{4,3,2,1,0:T(8,128)S(1)} collective-permute-done((f32[3,34,4,8,128]{4,3,2,1,0:T(8,128)}, f32[3,34,4,8,128]{4,3,2,1,0:T(8,128)S(1)}, u32[]{:S(2)}, u32[]{:S(2)}) %collective-permute-start.10) | collective-permute-done | bytes 1671200 | tf_op jit(solution)/shard_map/ppermute | solution.py:46
  392.7 176.6 %while.27 = (s32[]{:T(128)}, f32[16,2,3,8,128]{4,3,2,1,0:T(8,128)S(1)}, f32[16,2,3,112,128]{4,3,2,1,0:T(8,128)}, pred[16,2,16]{2,1,0:T(4,128)(4,1)S(1)}, s32[16,...) while((s32[]{:T(128)}, ...), condition=%wide.region_4.6_spmd, body=%wide.region_0.5_spmd.sunk | while | flops 57028160 | bytes 10317449 | solution.py:169
  398.3 4.1 fusion.123
  409.4 4.1 fusion.123
  420.4 4.1 fusion.123
  431.5 4.1 fusion.123
  442.5 4.1 fusion.123
  453.6 4.1 fusion.123
  464.6 4.1 fusion.123
  475.6 4.1 fusion.123
  486.7 4.1 fusion.123
  497.7 4.1 fusion.123
  508.7 4.1 fusion.123
  519.7 4.1 fusion.123
  530.8 4.1 fusion.123
  541.8 4.1 fusion.123
  563.9 4.1 fusion.123
  583.3 28.1 %collective-permute-done.11 = f32[3,34,3,8,128]{4,3,2,1,0:T(8,128)S(1)} collective-permute-done((f32[3,34,3,8,128]{4,3,2,1,0:T(8,128)S(1)}, f32[3,34,3,8,128]{4,3,2,1,0:T(8,128)S(1)}, u32[]{:S(2)}, u32[]{:S(2)}) %collective-permute-start.11) | collective-permute-done | bytes 1253408 | tf_op jit(solution)/shard_map/ppermute | solution.py:46
  615.4 5.6 collective-permute-done.12
  620.9 4.6 collective-permute-done.13
  (397 shorter events, 193.7 us)
Async XLA Ops:
  4.9 290.2 %copy-start.5 = (s32[1,1,32,1]{2,3,1,0:T(1,128)S(1)}, s32[1,1,32,1]{2,3,1,0:T(1,128)}, u32[]{:S(2)}) copy-start(s32[1,1,32,1]{2,3,1,0:T(1,128)} %param.67) | copy-start | bytes 388
  4.9 304.5 %copy-start.26 = (f32[7]{0:T(128)S(1)}, f32[7]{0:T(128)}, u32[]{:S(2)}) copy-start(f32[7]{0:T(128)} %constant.609.clone) | copy-start | bytes 88
  4.9 304.7 %copy-start.25 = (f32[7]{0:T(128)S(1)}, f32[7]{0:T(128)}, u32[]{:S(2)}) copy-start(f32[7]{0:T(128)} %constant.608.clone) | copy-start | bytes 88
  295.3 9.2 %collective-permute-start = (f32[1,1,32,7,1,128]{5,4,3,2,1,0:T(1,128)S(1)}, f32[1,1,32,7,1,128]{5,4,3,2,1,0:T(1,128)S(1)}, u32[]{:S(2)}, u32[]{:S(2)}) collective-permute-start(f32[1,1,32,7,1,128]{5,4,3,2,1,0:T(1,128)S(1)} %fusion.68), channel_id=1, source_target_pairs={{0,16},{16,32},{32,48},{48,64},{64,80},{80,96},{96,112},{112,128},... | collective-permute-start | bytes 344072 | tf_op jit(solution)/shard_map/ppermute | solution.py:38
  295.4 9.1 %collective-permute-start.1 = (f32[1,1,32,7,1,128]{5,4,3,2,1,0:T(1,128)S(1)}, f32[1,1,32,7,1,128]{5,4,3,2,1,0:T(1,128)S(1)}, u32[]{:S(2)}, u32[]{:S(2)}) collective-permute-start(f32[1,1,32,7,1,128]{5,4,3,2,1,0:T(1,128)S(1)} %fusion.68), channel_id=1, source_target_pairs={{16,0},{32,16},{48,32},{64,48},{80,64},{96,80},{112,96},{128,112},... | collective-permute-start | bytes 344072 | tf_op jit(solution)/shard_map/ppermute | solution.py:39
  304.9 18.0 %collective-permute-start.3 = (f32[3,1,32,7,1,128]{5,4,3,2,1,0:T(1,128)S(1)}, f32[3,1,32,7,1,128]{5,4,3,2,1,0:T(1,128)S(1)}, u32[]{:S(2)}, u32[]{:S(2)}) collective-permute-start(f32[3,1,32,7,1,128]{5,4,3,2,1,0:T(1,128)S(1)} %pad_maximum_fusion.9), channel_id=1, source_target_pairs={{4,0},{8,4},{12,8},{0,12},{5,1},{9,5},{13,9},{1,13},{6,2},{10,6},{... | collective-permute-start | bytes 1032200 | tf_op jit(solution)/shard_map/ppermute | solution.py:39
  305.0 17.9 %collective-permute-start.2 = (f32[3,1,32,7,1,128]{5,4,3,2,1,0:T(1,128)S(1)}, f32[3,1,32,7,1,128]{5,4,3,2,1,0:T(1,128)S(1)}, u32[]{:S(2)}, u32[]{:S(2)}) collective-permute-start(f32[3,1,32,7,1,128]{5,4,3,2,1,0:T(1,128)S(1)} %pad_maximum_fusion.9), channel_id=1, source_target_pairs={{0,4},{4,8},{8,12},{12,0},{1,5},{5,9},{9,13},{13,1},{2,6},{6,10},{... | collective-permute-start | bytes 1032200 | tf_op jit(solution)/shard_map/ppermute | solution.py:38
  322.9 4.0 collective-permute-start.4
  323.4 5.1 collective-permute-start.5
  328.6 41.9 %copy-start.6 = (s32[1,1,32,16]{2,3,1,0:T(8,128)S(1)}, s32[1,1,32,16]{2,3,1,0:T(8,128)}, u32[]{:S(2)}) copy-start(s32[1,1,32,16]{2,3,1,0:T(8,128)} %param.69) | copy-start | bytes 6148
  328.6 42.0 %copy-start.7 = (s32[1,1,32,16]{2,3,1,0:T(8,128)S(1)}, s32[1,1,32,16]{2,3,1,0:T(8,128)}, u32[]{:S(2)}) copy-start(s32[1,1,32,16]{2,3,1,0:T(8,128)} %param.70) | copy-start | bytes 6148
  328.6 42.1 %copy-start.27 = (s32[5]{0:T(128)S(1)}, s32[5]{0:T(128)}, u32[]{:S(2)}) copy-start(s32[5]{0:T(128)} %constant.604.clone.1) | copy-start | bytes 64
  330.4 42.4 %copy-start.20 = (f32[4]{0:T(128)S(1)}, f32[4]{0:T(128)}, u32[]{:S(2)}) copy-start(f32[4]{0:T(128)} %constant.615.clone) | copy-start | bytes 52
  331.5 23.4 %collective-permute-start.6 = (f32[1,32,4,8,128]{4,3,2,1,0:T(8,128)S(1)}, f32[1,32,4,8,128]{4,3,2,1,0:T(8,128)S(1)}, u32[]{:S(2)}, u32[]{:S(2)}) collective-permute-start(f32[1,32,4,8,128]{4,3,2,1,0:T(8,128)S(1)} %get-tuple-element.286), channel_id=1, source_target_pairs={{0,4},{4,8},{8,12},{12,0},{1,5},{5,9},{9,13},{13,1},{2,6},{6,10},{... | collective-permute-start | bytes 1572872 | tf_op jit(solution)/shard_map/ppermute | solution.py:38
  334.1 23.7 %collective-permute-start.7 = (f32[1,32,4,8,128]{4,3,2,1,0:T(8,128)S(1)}, f32[1,32,4,8,128]{4,3,2,1,0:T(8,128)S(1)}, u32[]{:S(2)}, u32[]{:S(2)}) collective-permute-start(f32[1,32,4,8,128]{4,3,2,1,0:T(8,128)S(1)} %get-tuple-element.286), channel_id=1, source_target_pairs={{4,0},{8,4},{12,8},{0,12},{5,1},{9,5},{13,9},{1,13},{6,2},{10,6},{... | collective-permute-start | bytes 1572872 | tf_op jit(solution)/shard_map/ppermute | solution.py:39
  357.8 5.4 collective-permute-start.8
  358.2 5.0 collective-permute-start.9
  364.5 23.3 %collective-permute-start.10 = (f32[3,34,4,8,128]{4,3,2,1,0:T(8,128)}, f32[3,34,4,8,128]{4,3,2,1,0:T(8,128)S(1)}, u32[]{:S(2)}, u32[]{:S(2)}) collective-permute-start(f32[3,34,4,8,128]{4,3,2,1,0:T(8,128)} %pad_maximum_fusion), channel_id=1, source_target_pairs={{0,240},{16,0},{32,16},{48,32},{64,48},{80,64},{96,80},{112,96},{1... | collective-permute-start | bytes 5013512 | tf_op jit(solution)/shard_map/ppermute | solution.py:46
  583.2 50.9 %copy-start.1 = (f32[32,7,8,128]{3,2,1,0:T(8,128)S(1)}, f32[32,7,8,128]{3,2,1,0:T(8,128)}, u32[]{:S(2)}) copy-start(f32[32,7,8,128]{3,2,1,0:T(8,128)} %copy-done) | copy-start | bytes 2752516
  583.2 28.2 %collective-permute-start.11 = (f32[3,34,3,8,128]{4,3,2,1,0:T(8,128)S(1)}, f32[3,34,3,8,128]{4,3,2,1,0:T(8,128)S(1)}, u32[]{:S(2)}, u32[]{:S(2)}) collective-permute-start(f32[3,34,3,8,128]{4,3,2,1,0:T(8,128)S(1)} %get-tuple-element.256), channel_id=1, source_target_pairs={{0,16},{16,32},{32,48},{48,64},{64,80},{80,96},{96,112},{112,128},... | collective-permute-start | bytes 3760136 | tf_op jit(solution)/shard_map/ppermute | solution.py:46
  611.6 9.4 %collective-permute-start.12 = (f32[1,34,3,8,128]{4,3,2,1,0:T(8,128)S(1)}, f32[1,34,3,8,128]{4,3,2,1,0:T(8,128)S(1)}, u32[]{:S(2)}, u32[]{:S(2)}) collective-permute-start(f32[1,34,3,8,128]{4,3,2,1,0:T(8,128)S(1)} %get-tuple-element.280), channel_id=1, source_target_pairs={{0,4},{4,8},{8,12},{12,0},{1,5},{5,9},{9,13},{13,1},{2,6},{6,10},{... | collective-permute-start | bytes 1253384 | tf_op jit(solution)/shard_map/ppermute | solution.py:38
  615.4 10.1 %collective-permute-start.13 = (f32[1,34,3,8,128]{4,3,2,1,0:T(8,128)S(1)}, f32[1,34,3,8,128]{4,3,2,1,0:T(8,128)S(1)}, u32[]{:S(2)}, u32[]{:S(2)}) collective-permute-start(f32[1,34,3,8,128]{4,3,2,1,0:T(8,128)S(1)} %get-tuple-element.281), channel_id=1, source_target_pairs={{4,0},{8,4},{12,8},{0,12},{5,1},{9,5},{13,9},{1,13},{6,2},{10,6},{... | collective-permute-start | bytes 1253384 | tf_op jit(solution)/shard_map/ppermute | solution.py:39
  625.5 4.8 collective-permute-start.14
  628.5 5.5 collective-permute-start.15
  (21 other events, 402.0 us)
where the time goes:
time: 639 us; the launch traced here: 637 us
  local copies, waits for them, and re-layouts  305 us (48%)
  other arithmetic  144 us (23%)
  waiting for transfers between devices  97.6 us (15%)
  matrix products  57.3 us (9%)
  starting transfers between devices  29.5 us (5%)
    gather x2, local copies, waits for them, and re-layouts, per_device(): jnp.take_along_axis(state, index, axis=2) * filled[:, None, :, None]  290 us
    reduce_sum x16, other arithmetic, tile_group(): on_right = -jnp.sum(push, axis=3)  65.7 us
    ppermute x2, waiting for transfers between devices, from_behind(): lax.ppermute(array, axis, [(i, (i + by) % size) for i in range(size)])  42.5 us
    reduce_sum x16, other arithmetic, tile_group(): dist = jnp.sum(diff * diff, axis=2)  33.2 us
    ppermute x7, waiting for transfers between devices, extended_2(): after = lax.ppermute(initial, axis, down)  28 us
    ppermute x7, waiting for transfers between devices, extended_2(): before = lax.ppermute(last, axis, up)  27 us
    dot_general x16, matrix products, tile_group(): jnp.einsum('cgp,cxpa->cgxa', hot_second, partner_block, precision=exact)  20.8 us
    dot_general x16, matrix products, tile_group(): other = jnp.einsum('cgp,cgxa->cxpa', hot_second, on_right, precision=exact)  18.7 us
  transfers between devices with their start and end apart: 16, of which 12 were waited for; matrix products, arithmetic and copies ran while one was open for 2% of the time, Pallas kernels for 0%

commit v1 on v0

v1 whole, which is shorter than its diff:
```python
import numpy as np
import jax
import jax.numpy as jnp
from jax import lax
from jax.experimental import pallas as pl
from jax.experimental.pallas import tpu as pltpu
from jax.sharding import PartitionSpec as P

FACES = ((-1, 0, 0), (1, 0, 0), (0, -1, 0), (0, 1, 0), (0, 0, -1), (0, 0, 1))
SHELL = (
    (0, 0, 0),
    (0, 0, 1),
    (0, 1, -1),
    (0, 1, 0),
    (0, 1, 1),
    (1, -1, -1),
    (1, -1, 0),
    (1, -1, 1),
    (1, 0, -1),
    (1, 0, 0),
    (1, 0, 1),
    (1, 1, -1),
    (1, 1, 0),
    (1, 1, 1),
)
STEP = 0.01
SOFTEN = 0.1
CELLS = 32
WIDE = CELLS + 4
ATOMS = 128
PAIRS = 16
NX, NY = 16, 4
LANES = 128
SEG = 40
ROW_LIVE, ROW_MIG, ROW_COUNT = 0, 1, 2
BEHIND = ((0, 0), (0, -1), (-1, 1), (-1, 0), (-1, -1))
NEAR = tuple((dx, dy) for dx in (-1, 0, 1) for dy in (-1, 0, 1))
MAX_TASKS = CELLS * PAIRS + len(BEHIND) * (CELLS + 2) * PAIRS

SMEM = pltpu.SMEM
VMEM = pltpu.VMEM
f32 = jnp.float32
i32 = jnp.int32

AT_S, AT_O, AT_T, AT_V, BUNDLE = 0, 128, 256, 272, 368
SHORT = AT_V
X1 = BUNDLE + 2 * SHORT + 128
X2 = 384
P_B, P_BP, P_BM, P_O2 = 0, BUNDLE, 2 * BUNDLE, 3 * BUNDLE
P_XP = P_O2 + 128
P_XM = P_XP + X1
P_X2P = P_XM + X1
P_X2M = P_X2P + X2
POOL = P_X2M + X2


def column_rows():
    at = {(0, 0): P_B, (0, 1): P_BP, (0, -1): P_BM}
    for dy in (-2, 2):
        at[0, dy] = P_O2 - 128
    for dx, x1, x2 in ((1, P_XP, P_X2P), (-1, P_XM, P_X2M)):
        at[dx, 0] = x1
        at[dx, 1] = x1 + BUNDLE
        at[dx, -1] = x1 + BUNDLE + SHORT
        for dy in (-2, 2):
            at[dx, dy] = x1 + BUNDLE + 2 * SHORT - 128
        at[2 * dx, 0] = x2 - 128
        at[2 * dx, 1] = x2
        at[2 * dx, -1] = x2 + 128
    return at


COLUMN = column_rows()
FAR = tuple(c for c in ((0, 2), (1, 2), (-1, 2), (2, 0), (2, 1), (2, -1), (-2, 0), (-2, 1), (-2, -1)))
E_T = 16 * len(NEAR) + 8 * len(FAR)
E_V = E_T + 16
EDGE = E_V + 8
EDGE_AT = {c: 16 * n for n, c in enumerate(NEAR)}
for _n, _c in enumerate(FAR):
    EDGE_AT[_c] = 16 * len(NEAR) + 8 * _n - 8
    if _c[1] == 2:
        EDGE_AT[_c[0], -2] = EDGE_AT[_c]


def moved_by(array, axis, by):
    size = lax.axis_size(axis)
    return lax.ppermute(array, axis, [(i, (i + by) % size) for i in range(size)])


def to_column(rows):
    pad = jnp.zeros((LANES - rows.shape[0], LANES), f32)
    return jnp.concatenate([rows, pad], axis=0).T


def pack_kernel(pos, stren, vel, first, second, live, mig, count, bundle, out_ref):
    bundle[AT_T : AT_T + 16, :] = jnp.zeros((16, LANES), f32)
    bundle[AT_T : AT_T + 16, 2 : 2 + CELLS] = first[...].astype(f32)
    bundle[AT_T : AT_T + 16, SEG + 2 : SEG + 2 + CELLS] = second[...].astype(f32)
    low = 2 * SEG + 2
    for row, ref in ((ROW_LIVE, live), (ROW_MIG, mig), (ROW_COUNT, count)):
        bundle[AT_T + row : AT_T + row + 1, low : low + CELLS] = ref[...].astype(f32)
    turned = to_column(bundle[AT_T : AT_T + 8, :])[low : low + CELLS, :]
    ids = jnp.broadcast_to(turned[:, ROW_MIG : ROW_MIG + 1], (CELLS, LANES))
    many = jnp.broadcast_to(turned[:, ROW_COUNT : ROW_COUNT + 1], (CELLS, LANES))
    low_slot = ids == 0.0
    kept = (1.0 - ids) < many
    filled = ids < many
    for c in range(4):
        if c < 3:
            one = pos[pl.ds(2 * c, CELLS, stride=6), :]
            two = pos[pl.ds(2 * c + 1, CELLS, stride=6), :]
        else:
            one = stren[pl.ds(0, CELLS, stride=2), :]
            two = stren[pl.ds(1, CELLS, stride=2), :]
        stay = jnp.where(kept, jnp.where(low_slot, two, one), 0.0)
        out = jnp.where(filled, jnp.where(low_slot, one, two), 0.0)
        bundle[pl.ds(AT_S + c, CELLS, stride=4), :] = stay
        bundle[pl.ds(AT_O + c, CELLS, stride=4), :] = out
        out_ref[pl.ds(c, CELLS, stride=4), :] = out
    for c in range(3):
        one = vel[pl.ds(2 * c, CELLS, stride=6), :]
        two = vel[pl.ds(2 * c + 1, CELLS, stride=6), :]
        speed = jnp.where(filled, jnp.where(low_slot, one, two), 0.0)
        bundle[pl.ds(AT_V + c, CELLS, stride=3), :] = speed


def place():
    return lax.axis_index("gx"), lax.axis_index("gy"), lax.axis_index("gz")


def heading_row(dest, x, y, dx, dy):
    row = lax.rem(x + (dx + NX), NX) * NY + lax.rem(y + (dy + NY), NY)
    return dest[pl.ds(row, 1), :]


def z_shift(z):
    return lax.rem(LANES + 2 - z * CELLS, LANES)


def iota(shape, axis):
    return lax.broadcasted_iota(i32, shape, axis)


def edges_kernel(b, bp, bm, o2, xp, xm, x2p, x2m, low, high):
    parts = (
        (P_B, b), (P_BP, bp), (P_BM, bm), (P_O2, o2),
        (P_XP, xp), (P_XM, xm), (P_X2P, x2p), (P_X2M, x2m),
    )

    def find(row):
        for start, ref in reversed(parts):
            if row >= start:
                return ref, row - start

    lane = iota((16, LANES), 1)
    for side, ref, cell in ((0, low, 0), (1, high, CELLS - 2)):
        table = jnp.zeros((16, LANES), f32)
        for n, column in enumerate(NEAR):
            source, row = find(COLUMN[column])
            to = EDGE_AT[column]
            ref[to : to + 8, :] = source[row + 4 * cell : row + 4 * cell + 8, :]
            row = row + 128
            ref[to + 8 : to + 16, :] = source[row + 4 * cell : row + 4 * cell + 8, :]
            values = source[row + 128 : row + 144, :]
            rolled = pltpu.roll(values, (2 * n - 2 - cell) % LANES, 1)
            for s in range(3):
                here = (lane >= s * SEG + 2 * n) & (lane < s * SEG + 2 * n + 2)
                table = jnp.where(here, rolled, table)
        for column in FAR:
            source, row = find(COLUMN[column] + 128)
            to = EDGE_AT[column] + 8
            ref[to : to + 8, :] = source[row + 4 * cell : row + 4 * cell + 8, :]
        ref[E_T : E_T + 16, :] = table
        at = AT_V + (88 if side else 0)
        ref[E_V : E_V + 8, :] = b[at : at + 8, :]


def find_tasks(dest, pool, edges, masks, words, heads, occ, turn):
    x, y, z = place()
    heads[...] = jnp.zeros_like(heads)
    for dx in range(-2, 3):
        for dy in range(-2, 3):
            if abs(dx) + abs(dy) < 4:
                at = (dx + 2) * 5 + dy + 2
                heads[at : at + 1, :] = heading_row(dest, x, y, dx, dy)
    heads[...] = pltpu.roll(heads[...], z_shift(z), 1)

    def head(dx, dy):
        at = (dx + 2) * 5 + dy + 2
        return heads[at : at + 1, :]

    slot = iota((PAIRS, LANES), 0)
    lane = iota((PAIRS, LANES), 1)
    thin = iota((1, LANES), 1)
    tables = {}
    for n, column in enumerate(NEAR):
        row = COLUMN[column] + AT_T
        values = pool[row : row + 16, :]
        if edges is not None:
            zlo, zhi = edges
            below = pltpu.roll(zlo[E_T : E_T + 16, :], (-2 * n) % LANES, 1)
            above = pltpu.roll(zhi[E_T : E_T + 16, :], (34 - 2 * n) % LANES, 1)
            for s in range(3):
                values = jnp.where((lane >= s * SEG) & (lane < s * SEG + 2), below, values)
                values = jnp.where((lane >= s * SEG + 34) & (lane < s * SEG + 36), above, values)
        tables[column] = values.astype(i32)
    rest = {c: pltpu.roll(tables[c], LANES - 2 * SEG, 1) for c in NEAR}
    ids = {c: rest[c][ROW_MIG : ROW_MIG + 1, :] for c in NEAR}
    counts = {c: rest[c][ROW_COUNT : ROW_COUNT + 1, :] for c in NEAR}
    filled = {c: (ids[c] < counts[c]).astype(i32) for c in NEAR}
    if edges is None:
        default = ((thin >= 2) & (thin < CELLS + 2)).astype(i32)
    else:
        default = jnp.ones((1, LANES), i32)

    def coming(dx, dy, face):
        return (head(dx, dy) == face).astype(i32) * filled.get((dx, dy), default)

    occ[...] = jnp.zeros_like(occ)
    turn[...] = jnp.zeros_like(turn)
    for n, (dx, dy) in enumerate(NEAR):
        turn[n : n + 1, :] = coming(dx, dy, 4) * 64
        turn[16 + n : 17 + n, :] = coming(dx, dy, 5) * 128
    from_below = pltpu.roll(turn[0:16, :], 1, 1)
    from_above = pltpu.roll(turn[16:32, :], LANES - 1, 1)
    for n, (dx, dy) in enumerate(NEAR):
        c = (dx, dy)
        kept0 = ((counts[c] > 0) & (ids[c] != 0)).astype(i32)
        kept1 = ((counts[c] > 1) & (ids[c] != 1)).astype(i32)
        sides = (
            coming(dx - 1, dy, 0) * 4
            + coming(dx + 1, dy, 1) * 8
            + coming(dx, dy - 1, 2) * 16
            + coming(dx, dy + 1, 3) * 32
        )
        occ[n : n + 1, :] = kept0 + 2 * kept1 + sides
    here = occ[...] + from_below + from_above
    by_z = {0: here, 1: pltpu.roll(here, LANES - 1, 1), -1: pltpu.roll(here, 1, 1)}

    def occupied(column, dz):
        n = NEAR.index(column)
        return jnp.broadcast_to(by_z[dz][n : n + 1, :], (PAIRS, LANES))

    def face_of(k):
        fx = jnp.where(k == 3, 1, jnp.where(k == 2, -1, 0))
        fy = jnp.where(k == 5, 1, jnp.where(k == 4, -1, 0))
        fz = jnp.where(k == 7, 1, jnp.where(k == 6, -1, 0))
        return fx, fy, fz

    def word_of(mine, target, theirs, at, vx, vy, vz, columns):
        half = (theirs >= 2).astype(i32)
        which = (vx + 2) * 5 + vy + 2
        inner = jnp.zeros_like(slot)
        outer = jnp.zeros_like(slot)
        for cx, cy in columns:
            same = which == (cx + 2) * 5 + cy + 2
            inner = jnp.where(same, COLUMN[cx, cy] // 4, inner)
            if edges is not None:
                outer = jnp.where(same, EDGE_AT[cx, cy] // 4, outer)
        entry = inner + 32 * half + at - 2
        if edges is not None:
            low_edge = outer + 2 * half + at + POOL // 4
            high_edge = outer + 2 * half + at - 34 + (POOL + EDGE) // 4
            entry = jnp.where(at < 2, low_edge, jnp.where(at >= CELLS + 2, high_edge, entry))
        return (
            entry
            + (target * 8 + mine) * 2048
            + ((vx + 2) + 8 * (vy + 2) + 64 * (vz + 2)) * (2048 * 256)
        )

    masks[...] = jnp.zeros_like(masks)
    power = lax.shift_left(jnp.ones_like(slot), slot)
    for g, column in enumerate(BEHIND):
        cx, cy = column
        inside = lane < WIDE
        first = jnp.where(inside, tables[column], 0)
        second = jnp.where(inside, pltpu.roll(tables[column], LANES - SEG, 1), 0)
        live = inside & (slot < rest[column][ROW_LIVE : ROW_LIVE + 1, :])
        block = lax.shift_right_logical(second, 3)
        part = second & 7
        there = live & ((lax.shift_right_logical(occupied(column, 0), first) & 1) == 1)
        if g == 0:
            left = jnp.zeros((PAIRS, LANES), i32)
            bx, by, bz = left, left, left
            for b, (ox, oy, oz) in enumerate(SHELL):
                same = block == b
                bit = lax.shift_right_logical(occupied((ox, oy), oz), part) & 1
                left = jnp.where(same, bit, left)
                bx = jnp.where(same, ox, bx)
                by = jnp.where(same, oy, by)
                bz = jnp.where(same, oz, bz)
            keep = there & (left == 1) & (lane >= 2) & (lane < CELLS + 2)
            fx, fy, fz = face_of(part)
            words[0:PAIRS, :] = word_of(
                first, lane - 2, part, lane + bz + fz, bx + fx, by + fy, bz + fz, COLUMN
            )
            masks[0:1, :] = jnp.sum(jnp.where(keep, power, 0), axis=0, keepdims=True)
        right = jnp.zeros((PAIRS, LANES), i32)
        bz = right
        for b, (ox, oy, oz) in enumerate(SHELL):
            if (ox, oy) == (-cx, -cy):
                same = block == b
                bit = lax.shift_right_logical(occupied((0, 0), oz), part) & 1
                within = (lane + oz >= 2) & (lane + oz < CELLS + 2)
                right = jnp.where(same & within, bit, right)
                bz = jnp.where(same, oz, bz)
        keep = there & (right == 1) & (first != second)
        fx, fy, fz = face_of(first)
        columns = [(cx + a, cy + b) for a, b in ((0, 0), (1, 0), (-1, 0), (0, 1), (0, -1))]
        words[PAIRS * (g + 1) : PAIRS * (g + 2), :] = word_of(
            part, lane + bz - 2, first, lane + fz, cx + fx, cy + fy, fz - bz, columns
        )
        masks[1 + g : 2 + g, :] = jnp.sum(jnp.where(keep, power, 0), axis=0, keepdims=True)


def list_tasks(masks, words, spots, tasks):
    def row_step(row, n):
        for lane in range(1, CELLS + 3):
            spots[n] = row * LANES + lane
            n = n + (masks[row, lane] != 0).astype(i32)
        return n

    many = lax.fori_loop(0, 6, row_step, jnp.int32(0))

    def spot_step(s, n):
        spot = spots[s]
        row = lax.shift_right_logical(spot, 7)
        lane = spot & (LANES - 1)
        mask = masks[row, lane]
        for p in range(PAIRS):
            tasks[n] = words[PAIRS * row + p, lane]
            n = n + (lax.shift_right_logical(mask, p) & 1)
        return n

    return lax.fori_loop(0, many, spot_step, jnp.int32(0))


def extend(dest, pool, vel, ext, heads):
    x, y, z = place()
    heads[0:8, :] = jnp.zeros((8, LANES), i32)
    spots = ((-1, 0), (1, 0), (0, -1), (0, 1), (0, 0))
    for n, (dx, dy) in enumerate(spots):
        heads[n : n + 1, :] = heading_row(dest, x, y, dx, dy)
    turned = pltpu.roll(heads[0:8, :], z_shift(z), 1)
    heads[0:8, :] = turned
    heads[5:6, :] = pltpu.roll(turned, LANES - 1, 1)[4:5, :]
    heads[4:5, :] = pltpu.roll(turned, 1, 1)[4:5, :]
    valid = (heads[0:8, :] == iota((8, LANES), 0)).astype(f32)
    full = to_column(valid)
    turned = to_column(pool[P_B + AT_T : P_B + AT_T + 8, :])[2 * SEG + 2 : 2 * SEG + 2 + CELLS, :]
    ids = jnp.broadcast_to(turned[:, ROW_MIG : ROW_MIG + 1], (CELLS, LANES))
    many = jnp.broadcast_to(turned[:, ROW_COUNT : ROW_COUNT + 1], (CELLS, LANES))
    for s in range(2):
        keep = (many > float(s)) & (ids != float(s))
        for r in range(7):
            if r < 3:
                value = pool[pl.ds(P_B + r, CELLS, stride=4), :]
            elif r == 6:
                value = pool[pl.ds(P_B + 3, CELLS, stride=4), :]
            else:
                value = vel[pl.ds(2 * (r - 3) + s, CELLS, stride=6), :]
            ext[pl.ds(8 * r + s, CELLS, stride=56), :] = jnp.where(keep, value, 0.0)
    bundles = (P_XM, P_XP, P_BM, P_BP, P_B, P_B)
    for f in range(6):
        flag = jnp.broadcast_to(full[2 : 2 + CELLS, f : f + 1], (CELLS, LANES))
        for r in range(7):
            shift = float(FACES[f][r]) if r < 3 else 0.0
            if 3 <= r < 6:
                at, step = bundles[f] + AT_V + r - 3, 3
            else:
                at, step = bundles[f] + AT_O + min(r, 3), 4
            inner = CELLS - 1
            if f < 4:
                value = (pool[pl.ds(at, CELLS, stride=step), :] + shift) * flag
                ext[pl.ds(8 * r + 2 + f, CELLS, stride=56), :] = value
            elif f == 4:
                value = (pool[pl.ds(at, inner, stride=step), :] + shift) * flag[1:CELLS, :]
                ext[pl.ds(56 + 8 * r + 6, inner, stride=56), :] = value
                ext[8 * r + 6 : 8 * r + 7, :] = jnp.zeros((1, LANES), f32)
            else:
                value = (pool[pl.ds(at + step, inner, stride=step), :] + shift) * flag[0:inner, :]
                ext[pl.ds(8 * r + 7, inner, stride=56), :] = value
                last = 56 * inner + 8 * r + 7
                ext[last : last + 1, :] = jnp.zeros((1, LANES), f32)


def patch(dest, zlo, zhi, ext):
    x, y, z = place()
    rows = jnp.broadcast_to(heading_row(dest, x, y, 0, 0), (8, LANES))
    rows = pltpu.roll(rows, z_shift(z), 1)[0:1, :]
    thin = iota((1, LANES), 1)
    up = jnp.sum(jnp.where((thin == 1) & (rows == 4), 1.0, 0.0), axis=1, keepdims=True)
    down = jnp.sum(jnp.where((thin == CELLS + 2) & (rows == 5), 1.0, 0.0), axis=1, keepdims=True)
    for ref, flag, cell, slot, at, speed_at, shift in (
        (zlo, up, 0, 6, EDGE_AT[0, 0] + 12, E_V + 5, -1.0),
        (zhi, down, CELLS - 1, 7, EDGE_AT[0, 0] + 8, E_V, 1.0),
    ):
        for r in range(7):
            row = speed_at + r - 3 if 3 <= r < 6 else at + min(r, 3)
            value = (ref[row : row + 1, :] + (shift if r == 2 else 0.0)) * flag
            to = 56 * cell + 8 * r + slot
            ext[to : to + 1, :] = value


def add_forces(tasks, many, pool, edges, ext, forces):
    def spread(entry, a):
        if edges is None:
            row = pool[pl.ds(4 * entry + a, 1), :]
        else:
            near = pool[pl.ds(4 * jnp.minimum(entry, POOL // 4 - 1) + a, 1), :]
            which = jnp.maximum(entry - POOL // 4, 0)
            zlo, zhi = edges
            below = zlo[pl.ds(4 * jnp.minimum(which, EDGE // 4 - 1) + a, 1), :]
            above = zhi[pl.ds(4 * jnp.maximum(which - EDGE // 4, 0) + a, 1), :]
            row = jnp.where(entry < POOL // 4, near, jnp.where(which < EDGE // 4, below, above))
        wide = jnp.broadcast_to(row, (8, LANES))
        return pltpu.roll(wide, 0, 1, stride=1, stride_axis=0)

    def step(t, _):
        code = tasks[t]
        entry = code & 2047
        target = lax.shift_right_logical(code, 11) & 255
        base = lax.shift_right_logical(target, 3) * 56 + (target & 7)
        away = lax.shift_right_logical(code, 19)
        sx, sy, sz, ss = (spread(entry, a) for a in range(4))
        ts = ext[pl.ds(base + 48, 1), :]
        goal = []
        for a in range(3):
            shift = ((lax.shift_right_logical(away, 3 * a) & 7) - 2).astype(f32)
            wide = jnp.broadcast_to(ext[pl.ds(base + 8 * a, 1), :], (8, LANES))
            goal.append(wide - shift)
        tx, ty, tz = goal
        fx = jnp.zeros((8, LANES), f32)
        fy, fz = fx, fx
        for j in range(LANES // 8):
            dx = tx - (pltpu.roll(sx, 8 * j, 1) if j else sx)
            dy = ty - (pltpu.roll(sy, 8 * j, 1) if j else sy)
            dz = tz - (pltpu.roll(sz, 8 * j, 1) if j else sz)
            strong = pltpu.roll(ss, 8 * j, 1) if j else ss
            dist = dx * dx + dy * dy + dz * dz
            reach = jnp.maximum(1.0 - dist, 0.0)
            weight = strong * reach * reach / (dist + SOFTEN)
            fx = fx + weight * dx
            fy = fy + weight * dy
            fz = fz + weight * dz
        to = lax.shift_right_logical(target, 3) * 24 + (target & 7)
        for a, part in enumerate((fx, fy, fz)):
            total = jnp.sum(part, axis=0, keepdims=True) * ts
            forces[pl.ds(to + 8 * a, 1), :] += total
        return 0

    lax.fori_loop(0, many, step, 0)


def to_scalars(masks, words, masks_s, words_s, sems):
    one = pltpu.make_async_copy(masks, masks_s, sems.at[0])
    two = pltpu.make_async_copy(words, words_s, sems.at[1])
    one.start()
    two.start()
    return one, two


def early_kernel(
    dest, vel, pool, ext, forces, masks, words, heads, occ, turn, masks_s, words_s, spots, tasks, sems
):
    find_tasks(dest, pool, None, masks, words, heads, occ, turn)
    copies = to_scalars(masks, words, masks_s, words_s, sems)
    extend(dest, pool, vel, ext, heads)
    forces[...] = jnp.zeros_like(forces)
    for copy in copies:
        copy.wait()
    many = list_tasks(masks_s, words_s, spots, tasks)
    add_forces(tasks, many, pool, None, ext, forces)


def late_kernel(
    dest, pool, zlo, zhi, ext_in, forces_in, done, moved, forces,
    ext, total, masks, words, heads, occ, turn, masks_s, words_s, spots, tasks, sems,
):
    find_tasks(dest, pool, (zlo, zhi), masks, words, heads, occ, turn)
    masks[...] = masks[...] & ~done[...]
    copies = to_scalars(masks, words, masks_s, words_s, sems)
    ext[...] = ext_in[...]
    total[...] = forces_in[...]
    patch(dest, zlo, zhi, ext)
    for copy in copies:
        copy.wait()
    many = list_tasks(masks_s, words_s, spots, tasks)
    add_forces(tasks, many, pool, (zlo, zhi), ext, total)

    def finish(cell, _):
        for a in range(3):
            force = total[pl.ds(pl.multiple_of(24 * cell + 8 * a, 8), 8), :]
            forces[0, 0, cell, a] = force
            speed = ext[pl.ds(pl.multiple_of(56 * cell + 24 + 8 * a, 8), 8), :] + STEP * force
            moved[0, 0, cell, 3 + a] = speed
            moved[0, 0, cell, a] = (
                ext[pl.ds(pl.multiple_of(56 * cell + 8 * a, 8), 8), :] + STEP * speed
            )
        return 0

    lax.fori_loop(0, CELLS, finish, 0)


def whole(space=VMEM):
    return pl.BlockSpec(memory_space=space)


def rows_of(n, dtype=f32):
    return jax.ShapeDtypeStruct((n, LANES), dtype)


def limit(mib):
    return pltpu.CompilerParams(vmem_limit_bytes=mib * 2**20)


LIST_SCRATCH = [
    VMEM((6 * PAIRS, LANES), i32),
    VMEM((32, LANES), i32),
    VMEM((16, LANES), i32),
    VMEM((32, LANES), i32),
    SMEM((8, LANES), i32),
    SMEM((6 * PAIRS, LANES), i32),
    SMEM((6 * LANES + 16,), i32),
    SMEM((MAX_TASKS + 16,), i32),
    pltpu.SemaphoreType.DMA((2,)),
]


def per_device(
    positions,
    velocities,
    strength,
    cluster_count,
    migrant_ids,
    destination,
    pair_i,
    pair_j,
    pair_count,
):
    pos = positions.reshape((CELLS * 6, ATOMS))
    vel = velocities.reshape((CELLS * 6, ATOMS))
    stren = strength.reshape((CELLS * 2, ATOMS))
    dest = destination.reshape((NX * NY, LANES))
    B, O = pl.pallas_call(
        pack_kernel,
        out_shape=[rows_of(BUNDLE), rows_of(128)],
        in_specs=[whole()] * 8,
        out_specs=[whole()] * 2,
        compiler_params=limit(8),
        name="pack",
    )(
        pos, stren, vel, pair_i[0, 0].T, pair_j[0, 0].T,
        pair_count.reshape((1, CELLS)), migrant_ids.reshape((1, CELLS)), cluster_count.reshape((1, CELLS)),
    )
    cat = jnp.concatenate
    B_p, B_m, O_2 = moved_by(B, "gy", -1), moved_by(B, "gy", 1), moved_by(O, "gy", 2)
    near = cat([B, B_p[:SHORT], B_m[:SHORT], O_2], axis=0)
    far = cat([O, B_p[AT_O:AT_T], B_m[AT_O:AT_T]], axis=0)
    X_p, X_m = moved_by(near, "gx", -1), moved_by(near, "gx", 1)
    X2_p, X2_m = moved_by(far, "gx", -2), moved_by(far, "gx", 2)
    buffers = (B, B_p, B_m, O_2, X_p, X_m, X2_p, X2_m)
    low, high = pl.pallas_call(
        edges_kernel,
        out_shape=[rows_of(EDGE), rows_of(EDGE)],
        in_specs=[whole()] * 8,
        out_specs=[whole()] * 2,
        compiler_params=limit(8),
        name="edges",
    )(*buffers)
    zlo, zhi = moved_by(high, "gz", 1), moved_by(low, "gz", -1)
    pool = cat(buffers, axis=0)
    ext, early, done = pl.pallas_call(
        early_kernel,
        out_shape=[rows_of(CELLS * 56), rows_of(CELLS * 24), rows_of(8, i32)],
        in_specs=[whole()] * 3,
        out_specs=[whole()] * 3,
        scratch_shapes=LIST_SCRATCH,
        compiler_params=limit(16),
        name="early",
    )(dest, vel, pool)
    return pl.pallas_call(
        late_kernel,
        out_shape=[
            jax.ShapeDtypeStruct((1, 1, CELLS, 6, 8, LANES), f32),
            jax.ShapeDtypeStruct((1, 1, CELLS, 3, 8, LANES), f32),
        ],
        in_specs=[whole()] * 7,
        out_specs=[whole()] * 2,
        scratch_shapes=[VMEM((CELLS * 56, LANES), f32), VMEM((CELLS * 24, LANES), f32), VMEM((8, LANES), i32)]
        + LIST_SCRATCH,
        compiler_params=limit(16),
        name="late",
    )(dest, pool, zlo, zhi, ext, early, done)


def solution(mesh):
    in_specs = (
        P("gx", "gy", "gz", None, None, None),
        P("gx", "gy", "gz", None, None, None),
        P("gx", "gy", "gz", None, None),
        P("gx", "gy", "gz"),
        P("gx", "gy", "gz", None),
        P(),
        P("gx", "gy", "gz", None),
        P("gx", "gy", "gz", None),
        P("gx", "gy", "gz"),
    )
    out_specs = (P("gx", "gy", "gz", None, None, None), P("gx", "gy", "gz", None, None, None))
    return jax.shard_map(
        per_device, mesh=mesh, in_specs=in_specs, out_specs=out_specs, check_vma=False
    )
```

time: 639 us -> 62.9 us (0.10)
  the two profiles are of different devices: /device:TPU:70 before, /device:TPU:1 now
where the time goes in v1:
time: 62.9 us; the launch traced here: 62.2 us
  starting transfers between devices  24 us (38%)
  waiting for transfers between devices  17.4 us (28%)
  Pallas kernels  13.9 us (22%)
  local copies, waits for them, and re-layouts  6.09 us (10%)
  between operations  0.81 us (1%)
    ppermute x9, starting transfers between devices, moved_by(): lax.ppermute(array, axis, [(i, (i + by) % size) for i in range(size)])  24 us
    ppermute x9, waiting for transfers between devices, moved_by(): lax.ppermute(array, axis, [(i, (i + by) % size) for i in range(size)])  17.4 us
    pallas_call x1, Pallas kernels, per_device(): pl.pallas_call(early_kernel, out_shape=[rows_of(CELLS * 56), rows_of(CELL...  9.89 us
    unnamed x27, local copies, waits for them, and re-layouts  6.05 us
    pallas_call x1, Pallas kernels, per_device(): pl.pallas_call(late_kernel, out_shape=[jax.ShapeDtypeStruct((1, 1, CELLS,...  3.62 us
  transfers between devices with their start and end apart: 9, of which 5 were waited for; matrix products, arithmetic and copies ran while one was open for 0% of the time, Pallas kernels for 16%

profile of v1, /device:TPU:1, one launch (start us, length us, event | category | flops | bytes accessed | tf_op | source)
XLA Modules:
  0.0 62.2 jit_solution(2282711957948521718)
XLA Ops:
  0.6 0.9 %copy-done = f32[1,1,32,3,2,128]{5,4,3,2,1,0:T(2,128)S(1)} copy-done((f32[1,1,32,3,2,128]{5,4,3,2,1,0:T(2,128)S(1)}, f32[1,1,32,3,2,128]{5,4,3,2,1,0:T(2,128)}, u32[]{:S(2)}) %copy-start) | copy-done | bytes 98328
  1.5 0.9 %copy-done.3 = f32[1,1,32,3,2,128]{5,4,3,2,1,0:T(2,128)S(1)} copy-done((f32[1,1,32,3,2,128]{5,4,3,2,1,0:T(2,128)S(1)}, f32[1,1,32,3,2,128]{5,4,3,2,1,0:T(2,128)}, u32[]{:S(2)}) %copy-start.3) | copy-done | bytes 98328
  2.4 0.8 %copy-done.4 = f32[1,1,32,2,128]{4,3,2,1,0:T(2,128)S(1)} copy-done((f32[1,1,32,2,128]{4,3,2,1,0:T(2,128)S(1)}, f32[1,1,32,2,128]{4,3,2,1,0:T(2,128)}, u32[]{:S(2)}) %copy-start.4) | copy-done | bytes 32792
  3.2 0.7 %copy-done.5 = s32[1,1,32,16]{2,3,1,0:T(8,128)S(1)} copy-done((s32[1,1,32,16]{2,3,1,0:T(8,128)S(1)}, s32[1,1,32,16]{2,3,1,0:T(8,128)}, u32[]{:S(2)}) %copy-start.5) | copy-done | bytes 2072
  3.9 0.7 %copy-done.6 = s32[1,1,32,16]{2,3,1,0:T(8,128)S(1)} copy-done((s32[1,1,32,16]{2,3,1,0:T(8,128)S(1)}, s32[1,1,32,16]{2,3,1,0:T(8,128)}, u32[]{:S(2)}) %copy-start.6) | copy-done | bytes 2072
  4.6 0.7 %copy-done.7 = s32[1,1,32]{2,1,0:T(1,128)S(1)} copy-done((s32[1,1,32]{2,1,0:T(1,128)S(1)}, s32[1,1,32]{2,1,0:T(1,128)}, u32[]{:S(2)}) %copy-start.7) | copy-done | bytes 152
  5.2 0.7 %copy-done.8 = s32[1,1,32,1]{2,3,1,0:T(1,128)S(1)} copy-done((s32[1,1,32,1]{2,3,1,0:T(1,128)S(1)}, s32[1,1,32,1]{2,3,1,0:T(1,128)}, u32[]{:S(2)}) %copy-start.8) | copy-done | bytes 152
  5.9 0.7 %copy-done.9 = s32[1,1,32]{2,1,0:T(1,128)S(1)} copy-done((s32[1,1,32]{2,1,0:T(1,128)S(1)}, s32[1,1,32]{2,1,0:T(1,128)}, u32[]{:S(2)}) %copy-start.9) | copy-done | bytes 152
  6.5 0.3 pack.1
  6.8 6.9 %collective-permute-start = (f32[368,128]{1,0:T(8,128)S(1)}, f32[368,128]{1,0:T(8,128)S(1)}, u32[]{:S(2)}, u32[]{:S(2)}) collective-permute-start(f32[368,128]{1,0:T(8,128)S(1)} %get-tuple-element.9.b), channel_id=1, source_target_pairs={{0,12},{4,0},{8,4},{12,8},{1,13},{5,1},{9,5},{13,9},{2,14},{6,2},{... | collective-permute-start | bytes 565256 | tf_op jit(solution)/shard_map/ppermute | solution.py:87
  13.7 3.3 %collective-permute-start.2 = (f32[128,128]{1,0:T(8,128)S(1)}, f32[128,128]{1,0:T(8,128)S(1)}, u32[]{:S(2)}, u32[]{:S(2)}) collective-permute-start(f32[128,128]{1,0:T(8,128)S(1)} %get-tuple-element.10), channel_id=1, source_target_pairs={{0,8},{4,12},{8,0},{12,4},{1,9},{5,13},{9,1},{13,5},{2,10},{6,14},... | collective-permute-start | bytes 196616 | tf_op jit(solution)/shard_map/ppermute | solution.py:87
  17.0 2.3 %collective-permute-done.bp = f32[368,128]{1,0:T(8,128)S(1)} collective-permute-done((f32[368,128]{1,0:T(8,128)S(1)}, f32[368,128]{1,0:T(8,128)S(1)}, u32[]{:S(2)}, u32[]{:S(2)}) %collective-permute-start) | collective-permute-done | bytes 188448 | tf_op jit(solution)/shard_map/ppermute | solution.py:87
  19.3 3.2 %collective-permute-done.1.bm = f32[368,128]{1,0:T(8,128)S(1)} collective-permute-done((f32[368,128]{1,0:T(8,128)S(1)}, f32[368,128]{1,0:T(8,128)S(1)}, u32[]{:S(2)}, u32[]{:S(2)}) %collective-permute-start.1) | collective-permute-done | bytes 188448 | tf_op jit(solution)/shard_map/ppermute | solution.py:87
  22.5 1.3 %collective-permute-done.2.o2 = f32[128,128]{1,0:T(8,128)S(1)} collective-permute-done((f32[128,128]{1,0:T(8,128)S(1)}, f32[128,128]{1,0:T(8,128)S(1)}, u32[]{:S(2)}, u32[]{:S(2)}) %collective-permute-start.2) | collective-permute-done | bytes 65568 | tf_op jit(solution)/shard_map/ppermute | solution.py:87
  23.8 5.0 %collective-permute-start.3 = (f32[1040,128]{1,0:T(8,128)S(1)}, f32[1040,128]{1,0:T(8,128)S(1)}, u32[]{:S(2)}, u32[]{:S(2)}) collective-permute-start(f32[1040,128]{1,0:T(8,128)S(1)} %pad_maximum_fusion), channel_id=1, source_target_pairs={{0,240},{16,0},{32,16},{48,32},{64,48},{80,64},{96,80},{112,96},{1... | collective-permute-start | bytes 1597448 | tf_op jit(solution)/shard_map/ppermute | solution.py:87
  28.8 1.3 %collective-permute-start.4 = (f32[1040,128]{1,0:T(8,128)S(1)}, f32[1040,128]{1,0:T(8,128)S(1)}, u32[]{:S(2)}, u32[]{:S(2)}) collective-permute-start(f32[1040,128]{1,0:T(8,128)S(1)} %pad_maximum_fusion), channel_id=1, source_target_pairs={{0,16},{16,32},{32,48},{48,64},{64,80},{80,96},{96,112},{112,128},... | collective-permute-start | bytes 1597448 | tf_op jit(solution)/shard_map/ppermute | solution.py:87
  30.2 4.7 %collective-permute-start.5 = (f32[384,128]{1,0:T(8,128)S(1)}, f32[384,128]{1,0:T(8,128)S(1)}, u32[]{:S(2)}, u32[]{:S(2)}) collective-permute-start(f32[384,128]{1,0:T(8,128)S(1)} %pad_maximum_fusion.1), channel_id=1, source_target_pairs={{0,224},{16,240},{32,0},{48,16},{64,32},{80,48},{96,64},{112,80},{... | collective-permute-start | bytes 589832 | tf_op jit(solution)/shard_map/ppermute | solution.py:87
  35.0 4.7 %collective-permute-done.5.x2p = f32[384,128]{1,0:T(8,128)S(1)} collective-permute-done((f32[384,128]{1,0:T(8,128)S(1)}, f32[384,128]{1,0:T(8,128)S(1)}, u32[]{:S(2)}, u32[]{:S(2)}) %collective-permute-start.5) | collective-permute-done | bytes 196640 | tf_op jit(solution)/shard_map/ppermute | solution.py:87
  39.7 5.9 %collective-permute-done.6.x2m = f32[384,128]{1,0:T(8,128)S(1)} collective-permute-done((f32[384,128]{1,0:T(8,128)S(1)}, f32[384,128]{1,0:T(8,128)S(1)}, u32[]{:S(2)}, u32[]{:S(2)}) %collective-permute-start.6) | collective-permute-done | bytes 196640 | tf_op jit(solution)/shard_map/ppermute | solution.py:87
  45.7 0.1 edges.1
  45.8 1.3 %collective-permute-start.7 = (f32[240,128]{1,0:T(8,128)S(1)}, f32[240,128]{1,0:T(8,128)S(1)}, u32[]{:S(2)}, u32[]{:S(2)}) collective-permute-start(f32[240,128]{1,0:T(8,128)S(1)} %get-tuple-element.11), channel_id=1, source_target_pairs={{0,1},{1,2},{2,3},{3,0},{4,5},{5,6},{6,7},{7,4},{8,9},{9,10},{10,1... | collective-permute-start | bytes 368648 | tf_op jit(solution)/shard_map/ppermute | solution.py:87
  47.1 1.5 %collective-permute-start.8 = (f32[240,128]{1,0:T(8,128)S(1)}, f32[240,128]{1,0:T(8,128)S(1)}, u32[]{:S(2)}, u32[]{:S(2)}) collective-permute-start(f32[240,128]{1,0:T(8,128)S(1)} %get-tuple-element.12), channel_id=1, source_target_pairs={{0,3},{1,0},{2,1},{3,2},{4,7},{5,4},{6,5},{7,6},{8,11},{9,8},{10,9... | collective-permute-start | bytes 368648 | tf_op jit(solution)/shard_map/ppermute | solution.py:87
  48.7 9.9 %early.1 = (f32[1792,128]{1,0:T(8,128)S(1)}, f32[768,128]{1,0:T(8,128)S(1)}, s32[8,128]{1,0:T(8,128)S(1)}) custom-call(s32[64,128]{1,0:T(8,128)S(1)} %bitcast.15, f32[192,128]{1,0:T(8,128)S(1)} %bitcast.14, f32[4080,128]{1,0:T(8,128)S(1)} %constant_dynamic-update-slice_fusion.pool), custom_call_target="tpu_custom_call" | custom-call | tf_op jit(solution)/shard_map/early/pallas_call | solution.py:573
  58.6 3.6 %late.1 = (f32[1,1,32,6,8,128]{5,4,3,2,1,0:T(8,128)}, f32[1,1,32,3,8,128]{5,4,3,2,1,0:T(8,128)}) custom-call(s32[64,128]{1,0:T(8,128)S(1)} %bitcast.16, f32[4080,128]{1,0:T(8,128)S(1)} %constant_dynamic-update-slice_fusion.pool, f32[240,128]{1,0:T(8,128)S(1)} %collective-permute-done.7.zlo, f32[240,128]{1,0:T(8,128)S(1)} %collective-permute-done.8.zhi, ...), custom_call_target="tpu_custom_call" | custom-call | tf_op jit(solution)/shard_map/late/pallas_call | solution.py:582
  (32 shorter events, 0.3 us)
Async XLA Ops:
  0.6 0.9 %copy-start = (f32[1,1,32,3,2,128]{5,4,3,2,1,0:T(2,128)S(1)}, f32[1,1,32,3,2,128]{5,4,3,2,1,0:T(2,128)}, u32[]{:S(2)}) copy-start(f32[1,1,32,3,2,128]{5,4,3,2,1,0:T(2,128)} %param.10) | copy-start | bytes 294916
  1.5 0.9 %copy-start.3 = (f32[1,1,32,3,2,128]{5,4,3,2,1,0:T(2,128)S(1)}, f32[1,1,32,3,2,128]{5,4,3,2,1,0:T(2,128)}, u32[]{:S(2)}) copy-start(f32[1,1,32,3,2,128]{5,4,3,2,1,0:T(2,128)} %param.9) | copy-start | bytes 294916
  2.4 0.8 %copy-start.4 = (f32[1,1,32,2,128]{4,3,2,1,0:T(2,128)S(1)}, f32[1,1,32,2,128]{4,3,2,1,0:T(2,128)}, u32[]{:S(2)}) copy-start(f32[1,1,32,2,128]{4,3,2,1,0:T(2,128)} %param.11) | copy-start | bytes 98308
  3.2 0.7 %copy-start.5 = (s32[1,1,32,16]{2,3,1,0:T(8,128)S(1)}, s32[1,1,32,16]{2,3,1,0:T(8,128)}, u32[]{:S(2)}) copy-start(s32[1,1,32,16]{2,3,1,0:T(8,128)} %param.15) | copy-start | bytes 6148
  3.9 0.7 %copy-start.6 = (s32[1,1,32,16]{2,3,1,0:T(8,128)S(1)}, s32[1,1,32,16]{2,3,1,0:T(8,128)}, u32[]{:S(2)}) copy-start(s32[1,1,32,16]{2,3,1,0:T(8,128)} %param.16) | copy-start | bytes 6148
  4.6 0.7 %copy-start.7 = (s32[1,1,32]{2,1,0:T(1,128)S(1)}, s32[1,1,32]{2,1,0:T(1,128)}, u32[]{:S(2)}) copy-start(s32[1,1,32]{2,1,0:T(1,128)} %param.17) | copy-start | bytes 388
  5.2 0.7 %copy-start.8 = (s32[1,1,32,1]{2,3,1,0:T(1,128)S(1)}, s32[1,1,32,1]{2,3,1,0:T(1,128)}, u32[]{:S(2)}) copy-start(s32[1,1,32,1]{2,3,1,0:T(1,128)} %param.13) | copy-start | bytes 388
  5.9 0.7 %copy-start.9 = (s32[1,1,32]{2,1,0:T(1,128)S(1)}, s32[1,1,32]{2,1,0:T(1,128)}, u32[]{:S(2)}) copy-start(s32[1,1,32]{2,1,0:T(1,128)} %param.12) | copy-start | bytes 388
  6.8 12.5 %collective-permute-start = (f32[368,128]{1,0:T(8,128)S(1)}, f32[368,128]{1,0:T(8,128)S(1)}, u32[]{:S(2)}, u32[]{:S(2)}) collective-permute-start(f32[368,128]{1,0:T(8,128)S(1)} %get-tuple-element.9.b), channel_id=1, source_target_pairs={{0,12},{4,0},{8,4},{12,8},{1,13},{5,1},{9,5},{13,9},{2,14},{6,2},{... | collective-permute-start | bytes 565256 | tf_op jit(solution)/shard_map/ppermute | solution.py:87
  13.7 8.7 %collective-permute-start.1 = (f32[368,128]{1,0:T(8,128)S(1)}, f32[368,128]{1,0:T(8,128)S(1)}, u32[]{:S(2)}, u32[]{:S(2)}) collective-permute-start(f32[368,128]{1,0:T(8,128)S(1)} %get-tuple-element.9.b), channel_id=1, source_target_pairs={{0,4},{4,8},{8,12},{12,0},{1,5},{5,9},{9,13},{13,1},{2,6},{6,10},{... | collective-permute-start | bytes 565256 | tf_op jit(solution)/shard_map/ppermute | solution.py:87
  13.7 10.1 %collective-permute-start.2 = (f32[128,128]{1,0:T(8,128)S(1)}, f32[128,128]{1,0:T(8,128)S(1)}, u32[]{:S(2)}, u32[]{:S(2)}) collective-permute-start(f32[128,128]{1,0:T(8,128)S(1)} %get-tuple-element.10), channel_id=1, source_target_pairs={{0,8},{4,12},{8,0},{12,4},{1,9},{5,13},{9,1},{13,5},{2,10},{6,14},... | collective-permute-start | bytes 196616 | tf_op jit(solution)/shard_map/ppermute | solution.py:87
  23.8 21.8 %collective-permute-start.3 = (f32[1040,128]{1,0:T(8,128)S(1)}, f32[1040,128]{1,0:T(8,128)S(1)}, u32[]{:S(2)}, u32[]{:S(2)}) collective-permute-start(f32[1040,128]{1,0:T(8,128)S(1)} %pad_maximum_fusion), channel_id=1, source_target_pairs={{0,240},{16,0},{32,16},{48,32},{64,48},{80,64},{96,80},{112,96},{1... | collective-permute-start | bytes 1597448 | tf_op jit(solution)/shard_map/ppermute | solution.py:87
  28.8 16.8 %collective-permute-start.4 = (f32[1040,128]{1,0:T(8,128)S(1)}, f32[1040,128]{1,0:T(8,128)S(1)}, u32[]{:S(2)}, u32[]{:S(2)}) collective-permute-start(f32[1040,128]{1,0:T(8,128)S(1)} %pad_maximum_fusion), channel_id=1, source_target_pairs={{0,16},{16,32},{32,48},{48,64},{64,80},{80,96},{96,112},{112,128},... | collective-permute-start | bytes 1597448 | tf_op jit(solution)/shard_map/ppermute | solution.py:87
  30.2 9.5 %collective-permute-start.5 = (f32[384,128]{1,0:T(8,128)S(1)}, f32[384,128]{1,0:T(8,128)S(1)}, u32[]{:S(2)}, u32[]{:S(2)}) collective-permute-start(f32[384,128]{1,0:T(8,128)S(1)} %pad_maximum_fusion.1), channel_id=1, source_target_pairs={{0,224},{16,240},{32,0},{48,16},{64,32},{80,48},{96,64},{112,80},{... | collective-permute-start | bytes 589832 | tf_op jit(solution)/shard_map/ppermute | solution.py:87
  34.9 10.7 %collective-permute-start.6 = (f32[384,128]{1,0:T(8,128)S(1)}, f32[384,128]{1,0:T(8,128)S(1)}, u32[]{:S(2)}, u32[]{:S(2)}) collective-permute-start(f32[384,128]{1,0:T(8,128)S(1)} %pad_maximum_fusion.1), channel_id=1, source_target_pairs={{0,32},{16,48},{32,64},{48,80},{64,96},{80,112},{96,128},{112,144}... | collective-permute-start | bytes 589832 | tf_op jit(solution)/shard_map/ppermute | solution.py:87
  35.0 13.7 %copy-start.1 = (f32[1,1,32,3,2,128]{5,4,3,2,1,0:T(2,128)S(1)}, f32[1,1,32,3,2,128]{5,4,3,2,1,0:T(2,128)}, u32[]{:S(2)}) copy-start(f32[1,1,32,3,2,128]{5,4,3,2,1,0:T(2,128)} %param.10) | copy-start | bytes 294916
  35.0 13.7 %copy-start.2 = (s32[16,4,128]{2,1,0:T(4,128)S(1)}, s32[16,4,128]{2,1,0:T(4,128)}, u32[]{:S(2)}) copy-start(s32[16,4,128]{2,1,0:T(4,128)} %param.14) | copy-start | bytes 98308
  45.8 12.8 %collective-permute-start.7 = (f32[240,128]{1,0:T(8,128)S(1)}, f32[240,128]{1,0:T(8,128)S(1)}, u32[]{:S(2)}, u32[]{:S(2)}) collective-permute-start(f32[240,128]{1,0:T(8,128)S(1)} %get-tuple-element.11), channel_id=1, source_target_pairs={{0,1},{1,2},{2,3},{3,0},{4,5},{5,6},{6,7},{7,4},{8,9},{9,10},{10,1... | collective-permute-start | bytes 368648 | tf_op jit(solution)/shard_map/ppermute | solution.py:87
  47.1 11.5 %collective-permute-start.8 = (f32[240,128]{1,0:T(8,128)S(1)}, f32[240,128]{1,0:T(8,128)S(1)}, u32[]{:S(2)}, u32[]{:S(2)}) collective-permute-start(f32[240,128]{1,0:T(8,128)S(1)} %get-tuple-element.12), channel_id=1, source_target_pairs={{0,3},{1,0},{2,1},{3,2},{4,7},{5,4},{6,5},{7,6},{8,11},{9,8},{10,9... | collective-permute-start | bytes 368648 | tf_op jit(solution)/shard_map/ppermute | solution.py:87

commit v2 on v1

--- a/solution.py
+++ b/solution.py
@@ -24,6 +24,7 @@
     (1, 1, 1),
 )
 STEP = 0.01
+EARLY_UNROLL, LATE_UNROLL = 8, 4
 SOFTEN = 0.1
 CELLS = 32
 WIDE = CELLS + 4
@@ -40,37 +41,31 @@
 SMEM = pltpu.SMEM
 VMEM = pltpu.VMEM
 f32 = jnp.float32
+bf16 = jnp.bfloat16
 i32 = jnp.int32
 
-AT_S, AT_O, AT_T, AT_V, BUNDLE = 0, 128, 256, 272, 368
-SHORT = AT_V
-X1 = BUNDLE + 2 * SHORT + 128
+OUT_T, AT_S, AT_V, BUNDLE = 128, 144, 272, 368
+X1 = BUNDLE + 2 * AT_V + 128
 X2 = 384
-P_B, P_BP, P_BM, P_O2 = 0, BUNDLE, 2 * BUNDLE, 3 * BUNDLE
-P_XP = P_O2 + 128
-P_XM = P_XP + X1
-P_X2P = P_XM + X1
-P_X2M = P_X2P + X2
-POOL = P_X2M + X2
+SIZES = (BUNDLE, BUNDLE, BUNDLE, 128, X1, X1, X2, X2)
+P_B, P_OP, P_OM, P_O2, P_XP, P_XM, P_X2P, P_X2M, POOL = (sum(SIZES[:n]) for n in range(len(SIZES) + 1))
 
 
 def column_rows():
-    at = {(0, 0): P_B, (0, 1): P_BP, (0, -1): P_BM}
+    out = {(0, 0): P_B, (0, 1): P_OP, (0, -1): P_OM}
+    for dx, x1, x2 in ((1, P_XP, P_X2P), (-1, P_XM, P_X2M)):
+        out[dx, 0], out[dx, 1], out[dx, -1] = x1, x1 + BUNDLE, x1 + BUNDLE + AT_V
+        for n, dy in enumerate((0, 1, -1)):
+            out[2 * dx, dy] = x2 + n * 128
+    stay = {c: at + AT_S for c, at in out.items() if abs(c[0]) < 2}
     for dy in (-2, 2):
-        at[0, dy] = P_O2 - 128
-    for dx, x1, x2 in ((1, P_XP, P_X2P), (-1, P_XM, P_X2M)):
-        at[dx, 0] = x1
-        at[dx, 1] = x1 + BUNDLE
-        at[dx, -1] = x1 + BUNDLE + SHORT
-        for dy in (-2, 2):
-            at[dx, dy] = x1 + BUNDLE + 2 * SHORT - 128
-        at[2 * dx, 0] = x2 - 128
-        at[2 * dx, 1] = x2
-        at[2 * dx, -1] = x2 + 128
-    return at
-
-
-COLUMN = column_rows()
+        out[0, dy] = P_O2
+        for dx, x1 in ((1, P_XP), (-1, P_XM)):
+            out[dx, dy] = x1 + BUNDLE + 2 * AT_V
+    return out, stay
+
+
+OUT_AT, STAY_AT = column_rows()
 FAR = tuple(c for c in ((0, 2), (1, 2), (-1, 2), (2, 0), (2, 1), (2, -1), (-2, 0), (-2, 1), (-2, -1)))
 E_T = 16 * len(NEAR) + 8 * len(FAR)
 E_V = E_T + 16
@@ -92,14 +87,21 @@
     return jnp.concatenate([rows, pad], axis=0).T
 
 
-def pack_kernel(pos, stren, vel, first, second, live, mig, count, bundle, out_ref):
-    bundle[AT_T : AT_T + 16, :] = jnp.zeros((16, LANES), f32)
-    bundle[AT_T : AT_T + 16, 2 : 2 + CELLS] = first[...].astype(f32)
-    bundle[AT_T : AT_T + 16, SEG + 2 : SEG + 2 + CELLS] = second[...].astype(f32)
+def pack_kernel(*refs):
+    sources, (bundle, alone), held, sems = refs[:8], refs[8:10], refs[10:18], refs[18]
+    copies = [pltpu.make_async_copy(a, b, sems.at[n]) for n, (a, b) in enumerate(zip(sources, held))]
+    for copy in copies:
+        copy.start()
+    for copy in copies:
+        copy.wait()
+    pos, stren, vel, first, second, live, mig, count = held
+    bundle[OUT_T : OUT_T + 16, :] = jnp.zeros((16, LANES), f32)
+    bundle[OUT_T : OUT_T + 16, 2 : 2 + CELLS] = first[...].astype(f32)
+    bundle[OUT_T : OUT_T + 16, SEG + 2 : SEG + 2 + CELLS] = second[...].astype(f32)
     low = 2 * SEG + 2
     for row, ref in ((ROW_LIVE, live), (ROW_MIG, mig), (ROW_COUNT, count)):
-        bundle[AT_T + row : AT_T + row + 1, low : low + CELLS] = ref[...].astype(f32)
-    turned = to_column(bundle[AT_T : AT_T + 8, :])[low : low + CELLS, :]
+        bundle[OUT_T + row : OUT_T + row + 1, low : low + CELLS] = ref[...].astype(f32)
+    turned = to_column(bundle[OUT_T : OUT_T + 8, :])[low : low + CELLS, :]
     ids = jnp.broadcast_to(turned[:, ROW_MIG : ROW_MIG + 1], (CELLS, LANES))
     many = jnp.broadcast_to(turned[:, ROW_COUNT : ROW_COUNT + 1], (CELLS, LANES))
     low_slot = ids == 0.0
@@ -115,8 +117,8 @@
         stay = jnp.where(kept, jnp.where(low_slot, two, one), 0.0)
         out = jnp.where(filled, jnp.where(low_slot, one, two), 0.0)
         bundle[pl.ds(AT_S + c, CELLS, stride=4), :] = stay
-        bundle[pl.ds(AT_O + c, CELLS, stride=4), :] = out
-        out_ref[pl.ds(c, CELLS, stride=4), :] = out
+        bundle[pl.ds(c, CELLS, stride=4), :] = out
+        alone[pl.ds(c, CELLS, stride=4), :] = out
     for c in range(3):
         one = vel[pl.ds(2 * c, CELLS, stride=6), :]
         two = vel[pl.ds(2 * c + 1, CELLS, stride=6), :]
@@ -141,9 +143,9 @@
     return lax.broadcasted_iota(i32, shape, axis)
 
 
-def edges_kernel(b, bp, bm, o2, xp, xm, x2p, x2m, low, high):
+def edges_kernel(b, op, om, o2, xp, xm, x2p, x2m, low, high):
     parts = (
-        (P_B, b), (P_BP, bp), (P_BM, bm), (P_O2, o2),
+        (P_B, b), (P_OP, op), (P_OM, om), (P_O2, o2),
         (P_XP, xp), (P_XM, xm), (P_X2P, x2p), (P_X2M, x2m),
     )
 
@@ -156,18 +158,18 @@
     for side, ref, cell in ((0, low, 0), (1, high, CELLS - 2)):
         table = jnp.zeros((16, LANES), f32)
         for n, column in enumerate(NEAR):
-            source, row = find(COLUMN[column])
+            source, row = find(OUT_AT[column])
             to = EDGE_AT[column]
-            ref[to : to + 8, :] = source[row + 4 * cell : row + 4 * cell + 8, :]
-            row = row + 128
+            first = row + AT_S + 4 * cell
+            ref[to : to + 8, :] = source[first : first + 8, :]
             ref[to + 8 : to + 16, :] = source[row + 4 * cell : row + 4 * cell + 8, :]
-            values = source[row + 128 : row + 144, :]
+            values = source[row + OUT_T : row + OUT_T + 16, :]
             rolled = pltpu.roll(values, (2 * n - 2 - cell) % LANES, 1)
             for s in range(3):
                 here = (lane >= s * SEG + 2 * n) & (lane < s * SEG + 2 * n + 2)
                 table = jnp.where(here, rolled, table)
         for column in FAR:
-            source, row = find(COLUMN[column] + 128)
+            source, row = find(OUT_AT[column])
             to = EDGE_AT[column] + 8
             ref[to : to + 8, :] = source[row + 4 * cell : row + 4 * cell + 8, :]
         ref[E_T : E_T + 16, :] = table
@@ -175,7 +177,7 @@
         ref[E_V : E_V + 8, :] = b[at : at + 8, :]
 
 
-def find_tasks(dest, pool, edges, masks, words, heads, occ, turn):
+def find_tasks(dest, near_tables, edges, masks, words, heads, occ, turn):
     x, y, z = place()
     heads[...] = jnp.zeros_like(heads)
     for dx in range(-2, 3):
@@ -194,8 +196,8 @@
     thin = iota((1, LANES), 1)
     tables = {}
     for n, column in enumerate(NEAR):
-        row = COLUMN[column] + AT_T
-        values = pool[row : row + 16, :]
+        ref, row = near_tables[column]
+        values = ref[row : row + 16, :]
         if edges is not None:
             zlo, zhi = edges
             below = pltpu.roll(zlo[E_T : E_T + 16, :], (-2 * n) % LANES, 1)
@@ -252,12 +254,15 @@
         which = (vx + 2) * 5 + vy + 2
         inner = jnp.zeros_like(slot)
         outer = jnp.zeros_like(slot)
+        stays = jnp.zeros_like(slot)
         for cx, cy in columns:
             same = which == (cx + 2) * 5 + cy + 2
-            inner = jnp.where(same, COLUMN[cx, cy] // 4, inner)
+            inner = jnp.where(same, OUT_AT[cx, cy] // 4, inner)
+            if (cx, cy) in STAY_AT:
+                stays = jnp.where(same, STAY_AT[cx, cy] // 4, stays)
             if edges is not None:
                 outer = jnp.where(same, EDGE_AT[cx, cy] // 4, outer)
-        entry = inner + 32 * half + at - 2
+        entry = jnp.where(half == 1, inner, stays) + at - 2
         if edges is not None:
             low_edge = outer + 2 * half + at + POOL // 4
             high_edge = outer + 2 * half + at - 34 + (POOL + EDGE) // 4
@@ -291,9 +296,9 @@
                 bz = jnp.where(same, oz, bz)
             keep = there & (left == 1) & (lane >= 2) & (lane < CELLS + 2)
             fx, fy, fz = face_of(part)
-            words[0:PAIRS, :] = word_of(
-                first, lane - 2, part, lane + bz + fz, bx + fx, by + fy, bz + fz, COLUMN
-            )
+            found = [word_of(
+                first, lane - 2, part, lane + bz + fz, bx + fx, by + fy, bz + fz, OUT_AT
+            )]
             masks[0:1, :] = jnp.sum(jnp.where(keep, power, 0), axis=0, keepdims=True)
         right = jnp.zeros((PAIRS, LANES), i32)
         bz = right
@@ -307,32 +312,63 @@
         keep = there & (right == 1) & (first != second)
         fx, fy, fz = face_of(first)
         columns = [(cx + a, cy + b) for a, b in ((0, 0), (1, 0), (-1, 0), (0, 1), (0, -1))]
-        words[PAIRS * (g + 1) : PAIRS * (g + 2), :] = word_of(
-            part, lane + bz - 2, first, lane + fz, cx + fx, cy + fy, fz - bz, columns
+        found.append(
+            word_of(part, lane + bz - 2, first, lane + fz, cx + fx, cy + fy, fz - bz, columns)
         )
         masks[1 + g : 2 + g, :] = jnp.sum(jnp.where(keep, power, 0), axis=0, keepdims=True)
-
-
-def list_tasks(masks, words, spots, tasks):
-    def row_step(row, n):
-        for lane in range(1, CELLS + 3):
-            spots[n] = row * LANES + lane
-            n = n + (masks[row, lane] != 0).astype(i32)
+    masks[7:8, :] = jnp.sum(masks[0:6, :], axis=0, keepdims=True)
+    for n in range(2):
+        one, two, three = found[3 * n : 3 * n + 3]
+        two, three = pltpu.roll(two, SEG, 1), pltpu.roll(three, 2 * SEG, 1)
+        packed = jnp.where(lane < SEG, one, jnp.where(lane < 2 * SEG, two, three))
+        words[PAIRS * n : PAIRS * (n + 1), :] = packed
+
+
+def lowest_bit(mask):
+    low = mask & -mask
+    at = jnp.int32(0)
+    for step, bits in ((8, 0xFF00), (4, 0xF0F0), (2, 0xCCCC), (1, 0xAAAA)):
+        at = at + jnp.where((low & bits) != 0, step, 0)
+    return at
+
+
+def list_tasks(masks, words, spots, tasks, ready):
+    many = jnp.int32(0)
+    for lane in range(1, CELLS + 3):
+        spots[many] = lane
+        many = many + (masks[7, lane] != 0).astype(i32)
+
+    def lane_step(s, n):
+        lane = spots[s]
+        for row in range(6):
+            mask = masks[row, lane]
+            spots[LANES + n] = mask
+            spots[8 * LANES + n] = row // 3 * PAIRS * LANES + row % 3 * SEG + lane
+            n = n + (mask != 0).astype(i32)
         return n
 
-    many = lax.fori_loop(0, 6, row_step, jnp.int32(0))
+    found = lax.fori_loop(0, many, lane_step, jnp.int32(0))
+    ready()
 
     def spot_step(s, n):
-        spot = spots[s]
+        spot = spots[8 * LANES + s]
         row = lax.shift_right_logical(spot, 7)
         lane = spot & (LANES - 1)
-        mask = masks[row, lane]
-        for p in range(PAIRS):
-            tasks[n] = words[PAIRS * row + p, lane]
-            n = n + (lax.shift_right_logical(mask, p) & 1)
-        return n
-
-    return lax.fori_loop(0, many, spot_step, jnp.int32(0))
+
+        def left(state):
+            return state[0] != 0
+
+        def take(state):
+            mask, n = state
+            tasks[n] = words[row + lowest_bit(mask), lane]
+            return mask & (mask - 1), n + 1
+
+        return lax.while_loop(left, take, take((spots[LANES + s], n)))[1]
+
+    n = lax.fori_loop(0, found, spot_step, jnp.int32(0))
+    for u in range(EARLY_UNROLL - 1):
+        tasks[n + u] = 0
+    return n
 
 
 def extend(dest, pool, vel, ext, heads):
@@ -347,28 +383,29 @@
     heads[4:5, :] = pltpu.roll(turned, 1, 1)[4:5, :]
     valid = (heads[0:8, :] == iota((8, LANES), 0)).astype(f32)
     full = to_column(valid)
-    turned = to_column(pool[P_B + AT_T : P_B + AT_T + 8, :])[2 * SEG + 2 : 2 * SEG + 2 + CELLS, :]
+    turned = to_column(pool[P_B + OUT_T : P_B + OUT_T + 8, :])
+    turned = turned[2 * SEG + 2 : 2 * SEG + 2 + CELLS, :]
     ids = jnp.broadcast_to(turned[:, ROW_MIG : ROW_MIG + 1], (CELLS, LANES))
     many = jnp.broadcast_to(turned[:, ROW_COUNT : ROW_COUNT + 1], (CELLS, LANES))
     for s in range(2):
         keep = (many > float(s)) & (ids != float(s))
         for r in range(7):
             if r < 3:
-                value = pool[pl.ds(P_B + r, CELLS, stride=4), :]
+                value = pool[pl.ds(P_B + AT_S + r, CELLS, stride=4), :]
             elif r == 6:
-                value = pool[pl.ds(P_B + 3, CELLS, stride=4), :]
+                value = pool[pl.ds(P_B + AT_S + 3, CELLS, stride=4), :]
             else:
                 value = vel[pl.ds(2 * (r - 3) + s, CELLS, stride=6), :]
             ext[pl.ds(8 * r + s, CELLS, stride=56), :] = jnp.where(keep, value, 0.0)
-    bundles = (P_XM, P_XP, P_BM, P_BP, P_B, P_B)
+    places = (P_XM, P_XP, P_OM, P_OP, P_B, P_B)
     for f in range(6):
         flag = jnp.broadcast_to(full[2 : 2 + CELLS, f : f + 1], (CELLS, LANES))
         for r in range(7):
             shift = float(FACES[f][r]) if r < 3 else 0.0
             if 3 <= r < 6:
-                at, step = bundles[f] + AT_V + r - 3, 3
+                at, step = places[f] + AT_V + r - 3, 3
             else:
-                at, step = bundles[f] + AT_O + min(r, 3), 4
+                at, step = places[f] + min(r, 3), 4
             inner = CELLS - 1
             if f < 4:
                 value = (pool[pl.ds(at, CELLS, stride=step), :] + shift) * flag
@@ -402,54 +439,100 @@
             ext[to : to + 1, :] = value
 
 
+def inverse(value):
+    return pl.reciprocal(value, approx=True)
+
+
+def split(value):
+    one = value.astype(bf16).astype(f32)
+    rest = value - one
+    two = rest.astype(bf16).astype(f32)
+    return one, two, rest - two
+
+
 def add_forces(tasks, many, pool, edges, ext, forces):
-    def spread(entry, a):
-        if edges is None:
-            row = pool[pl.ds(4 * entry + a, 1), :]
-        else:
-            near = pool[pl.ds(4 * jnp.minimum(entry, POOL // 4 - 1) + a, 1), :]
+    unroll = EARLY_UNROLL if edges is None else LATE_UNROLL
+    row = iota((8, LANES), 0)
+    top = row < 4
+    last = (row & 3) == 3
+
+    def source_of(entry):
+        near = pool[pl.ds(4 * jnp.minimum(entry, POOL // 4 - 1), 4), :]
+        if edges is not None:
             which = jnp.maximum(entry - POOL // 4, 0)
             zlo, zhi = edges
-            below = zlo[pl.ds(4 * jnp.minimum(which, EDGE // 4 - 1) + a, 1), :]
-            above = zhi[pl.ds(4 * jnp.maximum(which - EDGE // 4, 0) + a, 1), :]
-            row = jnp.where(entry < POOL // 4, near, jnp.where(which < EDGE // 4, below, above))
-        wide = jnp.broadcast_to(row, (8, LANES))
-        return pltpu.roll(wide, 0, 1, stride=1, stride_axis=0)
-
-    def step(t, _):
-        code = tasks[t]
+            below = zlo[pl.ds(4 * jnp.minimum(which, EDGE // 4 - 1), 4), :]
+            above = zhi[pl.ds(4 * jnp.maximum(which - EDGE // 4, 0), 4), :]
+            near = jnp.where(entry < POOL // 4, near, jnp.where(which < EDGE // 4, below, above))
+        return jnp.concatenate([near, near], axis=0)
+
+    def length(value):
+        return jnp.sum(jnp.where(top & ~last, value * value, 0.0), axis=0, keepdims=True)
+
+    def one(code, live):
         entry = code & 2047
         target = lax.shift_right_logical(code, 11) & 255
         base = lax.shift_right_logical(target, 3) * 56 + (target & 7)
         away = lax.shift_right_logical(code, 19)
-        sx, sy, sz, ss = (spread(entry, a) for a in range(4))
-        ts = ext[pl.ds(base + 48, 1), :]
-        goal = []
+        raw = source_of(entry)
+        source = jnp.where(last, raw, raw - 0.5)
+        goal = jnp.zeros((8, LANES), f32)
         for a in range(3):
             shift = ((lax.shift_right_logical(away, 3 * a) & 7) - 2).astype(f32)
             wide = jnp.broadcast_to(ext[pl.ds(base + 8 * a, 1), :], (8, LANES))
-            goal.append(wide - shift)
-        tx, ty, tz = goal
-        fx = jnp.zeros((8, LANES), f32)
-        fy, fz = fx, fx
-        for j in range(LANES // 8):
-            dx = tx - (pltpu.roll(sx, 8 * j, 1) if j else sx)
-            dy = ty - (pltpu.roll(sy, 8 * j, 1) if j else sy)
-            dz = tz - (pltpu.roll(sz, 8 * j, 1) if j else sz)
-            strong = pltpu.roll(ss, 8 * j, 1) if j else ss
-            dist = dx * dx + dy * dy + dz * dz
-            reach = jnp.maximum(1.0 - dist, 0.0)
-            weight = strong * reach * reach / (dist + SOFTEN)
-            fx = fx + weight * dx
-            fy = fy + weight * dy
-            fz = fz + weight * dz
+            goal = jnp.where((row & 3) == a, wide - shift - 0.5, goal)
+        strong = ext[pl.ds(base + 48, 1), :] * live
+        s1, s2, s3 = split(source)
+        t1, t2, t3 = split(goal)
+        a1, a2, a3 = split(jnp.broadcast_to(-length(source), (8, LANES)))
+        b1, b2, b3 = split(jnp.broadcast_to(1.0 - length(goal), (8, LANES)))
+        w1, w2, w3 = 2.0 * s1, 2.0 * s2, 2.0 * s3
+        left = jnp.concatenate(
+            [
+                jnp.where(last, jnp.where(top, a1, a2), jnp.where(top, w1, w2)),
+                jnp.where(last, 1.0, jnp.where(top, w1, w2)),
+                jnp.where(last, jnp.where(top, a3, 1.0), jnp.where(top, w1, w3)),
+                jnp.zeros((8, LANES), f32),
+            ],
+            axis=0,
+        ).astype(bf16)
+        right = jnp.concatenate(
+            [
+                jnp.where(last, 1.0, t1),
+                jnp.where(last, jnp.where(top, b1, b2), t2),
+                jnp.where(last, jnp.where(top, 1.0, b3), jnp.where(top, t3, t1)),
+                jnp.zeros((8, LANES), f32),
+            ],
+            axis=0,
+        ).astype(bf16)
+        inside = lax.dot_general(left, right, (((0,), (0,)), ((), ())), preferred_element_type=f32)
+        reach = jnp.maximum(inside, 0.0)
+        weight = reach * reach * inverse((1.0 + SOFTEN) - reach)
+        high = weight.astype(bf16)
+        low = (weight - high.astype(f32)).astype(bf16)
+        gain = jnp.broadcast_to(raw[3:4, :], (8, LANES))
+        v1, v2, v3 = split(jnp.where(last, gain, gain * source))
+        moment = jnp.concatenate([jnp.where(top, v1, v2), jnp.where(top, v3, 0.0)], axis=0).astype(bf16)
+        sums = jnp.dot(
+            jnp.concatenate([moment, moment], axis=1),
+            jnp.concatenate([high, low], axis=0),
+            preferred_element_type=f32,
+        )
+        sums = sums[0:8, :] + sums[8:16, :]
+        sums = sums[0:4, :] + sums[4:8, :]
+        push = (goal[0:4, :] * sums[3:4, :] - sums) * strong
         to = lax.shift_right_logical(target, 3) * 24 + (target & 7)
-        for a, part in enumerate((fx, fy, fz)):
-            total = jnp.sum(part, axis=0, keepdims=True) * ts
-            forces[pl.ds(to + 8 * a, 1), :] += total
+        return to, push
+
+    def step(t, _):
+        at = unroll * t
+        results = [one(tasks[at + u], (at + u < many).astype(f32)) for u in range(unroll)]
+        for to, push in results:
+            for a in range(3):
+                forces[pl.ds(to + 8 * a, 1), :] += push[a : a + 1, :]
         return 0
 
-    lax.fori_loop(0, many, step, 0)
+    lax.fori_loop(0, lax.div(many + (unroll - 1), unroll), step, 0)
 
 
 def to_scalars(masks, words, masks_s, words_s, sems):
@@ -460,32 +543,42 @@
     return one, two
 
 
+def flags_kernel(dest, b, op, om, xp, xm, masks, words, heads, occ, turn):
+    parts = ((P_B, b), (P_OP, op), (P_OM, om), (P_XP, xp), (P_XM, xm))
+    tables = {}
+    for column in NEAR:
+        row = OUT_AT[column] + OUT_T
+        start, ref = [part for part in parts if part[0] <= row][-1]
+        tables[column] = (ref, row - start)
+    find_tasks(dest, tables, None, masks, words, heads, occ, turn)
+
+
 def early_kernel(
-    dest, vel, pool, ext, forces, masks, words, heads, occ, turn, masks_s, words_s, spots, tasks, sems
+    dest, vel, pool, masks, words, ext, forces, heads, masks_s, words_s, spots, tasks, sems
 ):
-    find_tasks(dest, pool, None, masks, words, heads, occ, turn)
     copies = to_scalars(masks, words, masks_s, words_s, sems)
     extend(dest, pool, vel, ext, heads)
     forces[...] = jnp.zeros_like(forces)
-    for copy in copies:
-        copy.wait()
-    many = list_tasks(masks_s, words_s, spots, tasks)
+    copies[0].wait()
+    many = list_tasks(masks_s, words_s, spots, tasks, copies[1].wait)
     add_forces(tasks, many, pool, None, ext, forces)
 
 
 def late_kernel(
     dest, pool, zlo, zhi, ext_in, forces_in, done, moved, forces,
-    ext, total, masks, words, heads, occ, turn, masks_s, words_s, spots, tasks, sems,
+    ext, total, masks, words, occ, turn, heads, masks_s, words_s, spots, tasks, sems,
 ):
-    find_tasks(dest, pool, (zlo, zhi), masks, words, heads, occ, turn)
-    masks[...] = masks[...] & ~done[...]
+    tables = {c: (pool, OUT_AT[c] + OUT_T) for c in NEAR}
+    find_tasks(dest, tables, (zlo, zhi), masks, words, heads, occ, turn)
+    rest = masks[0:6, :] & ~done[0:6, :]
+    masks[0:6, :] = rest
+    masks[7:8, :] = jnp.sum(rest, axis=0, keepdims=True)
     copies = to_scalars(masks, words, masks_s, words_s, sems)
     ext[...] = ext_in[...]
     total[...] = forces_in[...]
     patch(dest, zlo, zhi, ext)
-    for copy in copies:
-        copy.wait()
-    many = list_tasks(masks_s, words_s, spots, tasks)
+    copies[0].wait()
+    many = list_tasks(masks_s, words_s, spots, tasks, copies[1].wait)
     add_forces(tasks, many, pool, (zlo, zhi), ext, total)
 
     def finish(cell, _):
@@ -514,14 +607,13 @@
     return pltpu.CompilerParams(vmem_limit_bytes=mib * 2**20)
 
 
+WORDS = 2 * PAIRS
+FIND_SCRATCH = [VMEM((16, LANES), i32), VMEM((32, LANES), i32)]
 LIST_SCRATCH = [
-    VMEM((6 * PAIRS, LANES), i32),
-    VMEM((32, LANES), i32),
-    VMEM((16, LANES), i32),
     VMEM((32, LANES), i32),
     SMEM((8, LANES), i32),
-    SMEM((6 * PAIRS, LANES), i32),
-    SMEM((6 * LANES + 16,), i32),
+    SMEM((WORDS, LANES), i32),
+    SMEM((16 * LANES,), i32),
     SMEM((MAX_TASKS + 16,), i32),
     pltpu.SemaphoreType.DMA((2,)),
 ]
@@ -545,18 +637,35 @@
     B, O = pl.pallas_call(
         pack_kernel,
         out_shape=[rows_of(BUNDLE), rows_of(128)],
-        in_specs=[whole()] * 8,
+        in_specs=[whole(pltpu.HBM)] * 8,
         out_specs=[whole()] * 2,
+        scratch_shapes=[
+            VMEM((CELLS * 6, ATOMS), f32),
+            VMEM((CELLS * 2, ATOMS), f32),
+            VMEM((CELLS * 6, ATOMS), f32),
+            VMEM((PAIRS, CELLS), i32),
+            VMEM((PAIRS, CELLS), i32),
+            VMEM((1, CELLS), i32),
+            VMEM((1, CELLS), i32),
+            VMEM((1, CELLS), i32),
+            pltpu.SemaphoreType.DMA((8,)),
+        ],
         compiler_params=limit(8),
         name="pack",
     )(
-        pos, stren, vel, pair_i[0, 0].T, pair_j[0, 0].T,
-        pair_count.reshape((1, CELLS)), migrant_ids.reshape((1, CELLS)), cluster_count.reshape((1, CELLS)),
+        *(
+            pltpu.with_memory_space_constraint(a, pltpu.HBM)
+            for a in (
+                pos, stren, vel, pair_i[0, 0].T, pair_j[0, 0].T,
+                pair_count.reshape((1, CELLS)), migrant_ids.reshape((1, CELLS)), cluster_count.reshape((1, CELLS)),
+            )
+        )
     )
     cat = jnp.concatenate
-    B_p, B_m, O_2 = moved_by(B, "gy", -1), moved_by(B, "gy", 1), moved_by(O, "gy", 2)
-    near = cat([B, B_p[:SHORT], B_m[:SHORT], O_2], axis=0)
-    far = cat([O, B_p[AT_O:AT_T], B_m[AT_O:AT_T]], axis=0)
+    O_2 = moved_by(O, "gy", 2)
+    B_p, B_m = moved_by(B, "gy", -1), moved_by(B, "gy", 1)
+    near = cat([B, B_p[:AT_V], B_m[:AT_V], O_2], axis=0)
+    far = cat([O, B_p[:128], B_m[:128]], axis=0)
     X_p, X_m = moved_by(near, "gx", -1), moved_by(near, "gx", 1)
     X2_p, X2_m = moved_by(far, "gx", -2), moved_by(far, "gx", 2)
     buffers = (B, B_p, B_m, O_2, X_p, X_m, X2_p, X2_m)
@@ -569,16 +678,25 @@
         name="edges",
     )(*buffers)
     zlo, zhi = moved_by(high, "gz", 1), moved_by(low, "gz", -1)
+    masks, words = pl.pallas_call(
+        flags_kernel,
+        out_shape=[rows_of(8, i32), rows_of(WORDS, i32)],
+        in_specs=[whole()] * 6,
+        out_specs=[whole()] * 2,
+        scratch_shapes=[VMEM((32, LANES), i32)] + FIND_SCRATCH,
+        compiler_params=limit(8),
+        name="flags",
+    )(dest, B, B_p, B_m, X_p, X_m)
     pool = cat(buffers, axis=0)
-    ext, early, done = pl.pallas_call(
+    ext, early = pl.pallas_call(
         early_kernel,
-        out_shape=[rows_of(CELLS * 56), rows_of(CELLS * 24), rows_of(8, i32)],
-        in_specs=[whole()] * 3,
-        out_specs=[whole()] * 3,
+        out_shape=[rows_of(CELLS * 56), rows_of(CELLS * 24)],
+        in_specs=[whole()] * 5,
+        out_specs=[whole()] * 2,
         scratch_shapes=LIST_SCRATCH,
         compiler_params=limit(16),
         name="early",
-    )(dest, vel, pool)
+    )(dest, vel, pool, masks, words)
     return pl.pallas_call(
         late_kernel,
         out_shape=[
@@ -587,11 +705,17 @@
         ],
         in_specs=[whole()] * 7,
         out_specs=[whole()] * 2,
-        scratch_shapes=[VMEM((CELLS * 56, LANES), f32), VMEM((CELLS * 24, LANES), f32), VMEM((8, LANES), i32)]
+        scratch_shapes=[
+            VMEM((CELLS * 56, LANES), f32),
+            VMEM((CELLS * 24, LANES), f32),
+            VMEM((8, LANES), i32),
+            VMEM((WORDS, LANES), i32),
+        ]
+        + FIND_SCRATCH
         + LIST_SCRATCH,
         compiler_params=limit(16),
         name="late",
-    )(dest, pool, zlo, zhi, ext, early, done)
+    )(dest, pool, zlo, zhi, ext, early, masks)
 
 
 def solution(mesh):

time: 62.9 us -> 50.8 us (0.81); the launches traced: 62.2 us -> 51 us
  local copies, waits for them, and re-layouts: 6.09 us -> 0.2 us
  Pallas kernels: 13.9 us -> 8.56 us
    pallas_call x1, Pallas kernels: 9.89 us -> 3.69 us  [per_device(): pl.pallas_call(early_kernel, out_shape=[rows_of(CELLS * 56), rows_of(CELL...]
    unnamed x27 -> x11, local copies, waits for them, and re-layouts: 6.05 us -> 0.15 us
    pallas_call x1, Pallas kernels: 0.27 us -> 1.31 us  [per_device(): pl.pallas_call(pack_kernel, out_shape=[rows_of(BUNDLE), rows_of(128)], in...]
  transfers between devices with their start and end apart: 9 -> 9, of which waited for: 5 -> 5; matrix products, arithmetic and copies ran while one was open for 0% -> 0% of each run, Pallas kernels for 16% -> 8%
where the time goes in v2:
time: 50.8 us; the launch traced here: 51 us
  starting transfers between devices  24 us (47%)
  waiting for transfers between devices  17.4 us (34%)
  Pallas kernels  8.56 us (17%)
  between operations  0.79 us (2%)
    ppermute x9, starting transfers between devices, moved_by(): lax.ppermute(array, axis, [(i, (i + by) % size) for i in range(size)])  24 us
    ppermute x9, waiting for transfers between devices, moved_by(): lax.ppermute(array, axis, [(i, (i + by) % size) for i in range(size)])  17.4 us
    pallas_call x1, Pallas kernels, per_device(): pl.pallas_call(early_kernel, out_shape=[rows_of(CELLS * 56), rows_of(CELL...  3.69 us
    pallas_call x1, Pallas kernels, per_device(): pl.pallas_call(late_kernel, out_shape=[jax.ShapeDtypeStruct((1, 1, CELLS,...  3.08 us
    pallas_call x1, Pallas kernels, per_device(): pl.pallas_call(pack_kernel, out_shape=[rows_of(BUNDLE), rows_of(128)], in...  1.31 us
  transfers between devices with their start and end apart: 9, of which 5 were waited for; matrix products, arithmetic and copies ran while one was open for 0% of the time, Pallas kernels for 8%

profile of v2, /device:TPU:1, one launch (start us, length us, event | category | flops | bytes accessed | tf_op | source)
XLA Modules:
  0.0 51.0 jit_solution(1764990297670145359)
XLA Ops:
  0.6 1.3 %pack.1 = (f32[368,128]{1,0:T(8,128)S(1)}, f32[128,128]{1,0:T(8,128)S(1)}) custom-call(f32[192,128]{1,0:T(8,128)} %bitcast.18, f32[64,128]{1,0:T(8,128)} %bitcast.19, f32[192,128]{1,0:T(8,128)} %bitcast.13, s32[16,32]{1,0:T(8,128)} %bitcast.20, s32[16,32]{1,0:T(8,128)} %bitcast.21, s32[1,32]{1,0:T(1,128)} %bitcast.22, s32[1,32]{1,0:T(1,128)} %bitcast.23, ...), custom_call_target="tpu_custom_call" | custom-call | tf_op jit(solution)/shard_map/pack/pallas_call | solution.py:637
  1.9 6.9 %collective-permute-start = (f32[368,128]{1,0:T(8,128)S(1)}, f32[368,128]{1,0:T(8,128)S(1)}, u32[]{:S(2)}, u32[]{:S(2)}) collective-permute-start(f32[368,128]{1,0:T(8,128)S(1)} %get-tuple-element.10.b), channel_id=1, source_target_pairs={{0,12},{4,0},{8,4},{12,8},{1,13},{5,1},{9,5},{13,9},{2,14},{6,2},{... | collective-permute-start | bytes 565256 | tf_op jit(solution)/shard_map/ppermute | solution.py:82
  8.9 0.0 collective-permute-start.1
  8.9 3.3 %collective-permute-start.2 = (f32[128,128]{1,0:T(8,128)S(1)}, f32[128,128]{1,0:T(8,128)S(1)}, u32[]{:S(2)}, u32[]{:S(2)}) collective-permute-start(f32[128,128]{1,0:T(8,128)S(1)} %get-tuple-element.11), channel_id=1, source_target_pairs={{0,8},{4,12},{8,0},{12,4},{1,9},{5,13},{9,1},{13,5},{2,10},{6,14},... | collective-permute-start | bytes 196616 | tf_op jit(solution)/shard_map/ppermute | solution.py:82
  12.1 2.3 %collective-permute-done.op = f32[368,128]{1,0:T(8,128)S(1)} collective-permute-done((f32[368,128]{1,0:T(8,128)S(1)}, f32[368,128]{1,0:T(8,128)S(1)}, u32[]{:S(2)}, u32[]{:S(2)}) %collective-permute-start) | collective-permute-done | bytes 188448 | tf_op jit(solution)/shard_map/ppermute | solution.py:82
  14.4 3.2 %collective-permute-done.1.om = f32[368,128]{1,0:T(8,128)S(1)} collective-permute-done((f32[368,128]{1,0:T(8,128)S(1)}, f32[368,128]{1,0:T(8,128)S(1)}, u32[]{:S(2)}, u32[]{:S(2)}) %collective-permute-start.1) | collective-permute-done | bytes 188448 | tf_op jit(solution)/shard_map/ppermute | solution.py:82
  17.6 1.3 %collective-permute-done.2.o2 = f32[128,128]{1,0:T(8,128)S(1)} collective-permute-done((f32[128,128]{1,0:T(8,128)S(1)}, f32[128,128]{1,0:T(8,128)S(1)}, u32[]{:S(2)}, u32[]{:S(2)}) %collective-permute-start.2) | collective-permute-done | bytes 65568 | tf_op jit(solution)/shard_map/ppermute | solution.py:82
  19.0 5.0 %collective-permute-start.3 = (f32[1040,128]{1,0:T(8,128)S(1)}, f32[1040,128]{1,0:T(8,128)S(1)}, u32[]{:S(2)}, u32[]{:S(2)}) collective-permute-start(f32[1040,128]{1,0:T(8,128)S(1)} %pad_maximum_fusion), channel_id=1, source_target_pairs={{0,240},{16,0},{32,16},{48,32},{64,48},{80,64},{96,80},{112,96},{1... | collective-permute-start | bytes 1597448 | tf_op jit(solution)/shard_map/ppermute | solution.py:82
  24.0 1.3 %collective-permute-start.4 = (f32[1040,128]{1,0:T(8,128)S(1)}, f32[1040,128]{1,0:T(8,128)S(1)}, u32[]{:S(2)}, u32[]{:S(2)}) collective-permute-start(f32[1040,128]{1,0:T(8,128)S(1)} %pad_maximum_fusion), channel_id=1, source_target_pairs={{0,16},{16,32},{32,48},{48,64},{64,80},{80,96},{96,112},{112,128},... | collective-permute-start | bytes 1597448 | tf_op jit(solution)/shard_map/ppermute | solution.py:82
  25.3 4.7 %collective-permute-start.5 = (f32[384,128]{1,0:T(8,128)S(1)}, f32[384,128]{1,0:T(8,128)S(1)}, u32[]{:S(2)}, u32[]{:S(2)}) collective-permute-start(f32[384,128]{1,0:T(8,128)S(1)} %pad_maximum_fusion.1), channel_id=1, source_target_pairs={{0,224},{16,240},{32,0},{48,16},{64,32},{80,48},{96,64},{112,80},{... | collective-permute-start | bytes 589832 | tf_op jit(solution)/shard_map/ppermute | solution.py:82
  30.1 0.0 collective-permute-start.6
  30.1 0.0 copy-start.1
  30.1 4.7 %collective-permute-done.5.x2p = f32[384,128]{1,0:T(8,128)S(1)} collective-permute-done((f32[384,128]{1,0:T(8,128)S(1)}, f32[384,128]{1,0:T(8,128)S(1)}, u32[]{:S(2)}, u32[]{:S(2)}) %collective-permute-start.5) | collective-permute-done | bytes 196640 | tf_op jit(solution)/shard_map/ppermute | solution.py:82
  34.8 5.9 %collective-permute-done.6.x2m = f32[384,128]{1,0:T(8,128)S(1)} collective-permute-done((f32[384,128]{1,0:T(8,128)S(1)}, f32[384,128]{1,0:T(8,128)S(1)}, u32[]{:S(2)}, u32[]{:S(2)}) %collective-permute-start.6) | collective-permute-done | bytes 196640 | tf_op jit(solution)/shard_map/ppermute | solution.py:82
  40.8 0.0 collective-permute-done.3.xp
  40.8 0.0 collective-permute-done.4.xm
  40.8 0.1 edges.1
  40.9 1.3 %collective-permute-start.7 = (f32[240,128]{1,0:T(8,128)S(1)}, f32[240,128]{1,0:T(8,128)S(1)}, u32[]{:S(2)}, u32[]{:S(2)}) collective-permute-start(f32[240,128]{1,0:T(8,128)S(1)} %get-tuple-element.12), channel_id=1, source_target_pairs={{0,1},{1,2},{2,3},{3,0},{4,5},{5,6},{6,7},{7,4},{8,9},{9,10},{10,1... | collective-permute-start | bytes 368648 | tf_op jit(solution)/shard_map/ppermute | solution.py:82
  42.2 1.5 %collective-permute-start.8 = (f32[240,128]{1,0:T(8,128)S(1)}, f32[240,128]{1,0:T(8,128)S(1)}, u32[]{:S(2)}, u32[]{:S(2)}) collective-permute-start(f32[240,128]{1,0:T(8,128)S(1)} %get-tuple-element.13), channel_id=1, source_target_pairs={{0,3},{1,0},{2,1},{3,2},{4,7},{5,4},{6,5},{7,6},{8,11},{9,8},{10,9... | collective-permute-start | bytes 368648 | tf_op jit(solution)/shard_map/ppermute | solution.py:82
  43.8 0.4 flags.1
  44.2 3.7 %early.1 = (f32[1792,128]{1,0:T(8,128)S(1)}, f32[768,128]{1,0:T(8,128)S(1)}) custom-call(s32[64,128]{1,0:T(8,128)S(1)} %bitcast.16, f32[192,128]{1,0:T(8,128)S(1)} %bitcast.14, f32[4080,128]{1,0:T(8,128)S(1)} %constant_dynamic-update-slice_fusion.pool, s32[8,128]{1,0:T(8,128)S(1)} %get-tuple-element.14.masks.done, s32[32,128]{1,0:T(8,128)S(1)} %get-tuple-element.15.words), custom_call_target="tpu_custom_call" | custom-call | tf_op jit(solution)/shard_map/early/pallas_call | solution.py:691
  47.9 0.0 collective-permute-done.7.zlo
  47.9 0.0 collective-permute-done.8.zhi
  47.9 3.1 %late.1 = (f32[1,1,32,6,8,128]{5,4,3,2,1,0:T(8,128)}, f32[1,1,32,3,8,128]{5,4,3,2,1,0:T(8,128)}) custom-call(s32[64,128]{1,0:T(8,128)S(1)} %bitcast.17, f32[4080,128]{1,0:T(8,128)S(1)} %constant_dynamic-update-slice_fusion.pool, f32[240,128]{1,0:T(8,128)S(1)} %collective-permute-done.7.zlo, f32[240,128]{1,0:T(8,128)S(1)} %collective-permute-done.8.zhi, ...), custom_call_target="tpu_custom_call" | custom-call | tf_op jit(solution)/shard_map/late/pallas_call | solution.py:700
  (17 shorter events, 0.2 us)
Async XLA Ops:
  1.9 12.5 %collective-permute-start = (f32[368,128]{1,0:T(8,128)S(1)}, f32[368,128]{1,0:T(8,128)S(1)}, u32[]{:S(2)}, u32[]{:S(2)}) collective-permute-start(f32[368,128]{1,0:T(8,128)S(1)} %get-tuple-element.10.b), channel_id=1, source_target_pairs={{0,12},{4,0},{8,4},{12,8},{1,13},{5,1},{9,5},{13,9},{2,14},{6,2},{... | collective-permute-start | bytes 565256 | tf_op jit(solution)/shard_map/ppermute | solution.py:82
  8.9 8.7 %collective-permute-start.1 = (f32[368,128]{1,0:T(8,128)S(1)}, f32[368,128]{1,0:T(8,128)S(1)}, u32[]{:S(2)}, u32[]{:S(2)}) collective-permute-start(f32[368,128]{1,0:T(8,128)S(1)} %get-tuple-element.10.b), channel_id=1, source_target_pairs={{0,4},{4,8},{8,12},{12,0},{1,5},{5,9},{9,13},{13,1},{2,6},{6,10},{... | collective-permute-start | bytes 565256 | tf_op jit(solution)/shard_map/ppermute | solution.py:82
  8.9 10.1 %collective-permute-start.2 = (f32[128,128]{1,0:T(8,128)S(1)}, f32[128,128]{1,0:T(8,128)S(1)}, u32[]{:S(2)}, u32[]{:S(2)}) collective-permute-start(f32[128,128]{1,0:T(8,128)S(1)} %get-tuple-element.11), channel_id=1, source_target_pairs={{0,8},{4,12},{8,0},{12,4},{1,9},{5,13},{9,1},{13,5},{2,10},{6,14},... | collective-permute-start | bytes 196616 | tf_op jit(solution)/shard_map/ppermute | solution.py:82
  19.0 21.8 %collective-permute-start.3 = (f32[1040,128]{1,0:T(8,128)S(1)}, f32[1040,128]{1,0:T(8,128)S(1)}, u32[]{:S(2)}, u32[]{:S(2)}) collective-permute-start(f32[1040,128]{1,0:T(8,128)S(1)} %pad_maximum_fusion), channel_id=1, source_target_pairs={{0,240},{16,0},{32,16},{48,32},{64,48},{80,64},{96,80},{112,96},{1... | collective-permute-start | bytes 1597448 | tf_op jit(solution)/shard_map/ppermute | solution.py:82
  24.0 16.8 %collective-permute-start.4 = (f32[1040,128]{1,0:T(8,128)S(1)}, f32[1040,128]{1,0:T(8,128)S(1)}, u32[]{:S(2)}, u32[]{:S(2)}) collective-permute-start(f32[1040,128]{1,0:T(8,128)S(1)} %pad_maximum_fusion), channel_id=1, source_target_pairs={{0,16},{16,32},{32,48},{48,64},{64,80},{80,96},{96,112},{112,128},... | collective-permute-start | bytes 1597448 | tf_op jit(solution)/shard_map/ppermute | solution.py:82
  25.3 9.5 %collective-permute-start.5 = (f32[384,128]{1,0:T(8,128)S(1)}, f32[384,128]{1,0:T(8,128)S(1)}, u32[]{:S(2)}, u32[]{:S(2)}) collective-permute-start(f32[384,128]{1,0:T(8,128)S(1)} %pad_maximum_fusion.1), channel_id=1, source_target_pairs={{0,224},{16,240},{32,0},{48,16},{64,32},{80,48},{96,64},{112,80},{... | collective-permute-start | bytes 589832 | tf_op jit(solution)/shard_map/ppermute | solution.py:82
  30.1 10.7 %collective-permute-start.6 = (f32[384,128]{1,0:T(8,128)S(1)}, f32[384,128]{1,0:T(8,128)S(1)}, u32[]{:S(2)}, u32[]{:S(2)}) collective-permute-start(f32[384,128]{1,0:T(8,128)S(1)} %pad_maximum_fusion.1), channel_id=1, source_target_pairs={{0,32},{16,48},{32,64},{48,80},{64,96},{80,112},{96,128},{112,144}... | collective-permute-start | bytes 589832 | tf_op jit(solution)/shard_map/ppermute | solution.py:82
  30.1 13.7 %copy-start.1 = (s32[16,4,128]{2,1,0:T(4,128)S(1)}, s32[16,4,128]{2,1,0:T(4,128)}, u32[]{:S(2)}) copy-start(s32[16,4,128]{2,1,0:T(4,128)} %param.14) | copy-start | bytes 98308
  40.9 7.0 %collective-permute-start.7 = (f32[240,128]{1,0:T(8,128)S(1)}, f32[240,128]{1,0:T(8,128)S(1)}, u32[]{:S(2)}, u32[]{:S(2)}) collective-permute-start(f32[240,128]{1,0:T(8,128)S(1)} %get-tuple-element.12), channel_id=1, source_target_pairs={{0,1},{1,2},{2,3},{3,0},{4,5},{5,6},{6,7},{7,4},{8,9},{9,10},{10,1... | collective-permute-start | bytes 368648 | tf_op jit(solution)/shard_map/ppermute | solution.py:82
  42.2 2.0 %copy-start = (f32[1,1,32,3,2,128]{5,4,3,2,1,0:T(2,128)S(1)}, f32[1,1,32,3,2,128]{5,4,3,2,1,0:T(2,128)}, u32[]{:S(2)}) copy-start(f32[1,1,32,3,2,128]{5,4,3,2,1,0:T(2,128)} %param.10) | copy-start | bytes 294916
  42.2 5.7 %collective-permute-start.8 = (f32[240,128]{1,0:T(8,128)S(1)}, f32[240,128]{1,0:T(8,128)S(1)}, u32[]{:S(2)}, u32[]{:S(2)}) collective-permute-start(f32[240,128]{1,0:T(8,128)S(1)} %get-tuple-element.13), channel_id=1, source_target_pairs={{0,3},{1,0},{2,1},{3,2},{4,7},{5,4},{6,5},{7,6},{8,11},{9,8},{10,9... | collective-permute-start | bytes 368648 | tf_op jit(solution)/shard_map/ppermute | solution.py:82

commit v3 on v2

--- a/solution.py
+++ b/solution.py
@@ -44,24 +44,27 @@
 bf16 = jnp.bfloat16
 i32 = jnp.int32
 
-OUT_T, AT_S, AT_V, BUNDLE = 128, 144, 272, 368
-X1 = BUNDLE + 2 * AT_V + 128
+OUT_T, AT_S, BUNDLE = 128, 144, 272
+SPEEDS = 96
+X1 = 3 * BUNDLE + 128 + SPEEDS
 X2 = 384
-SIZES = (BUNDLE, BUNDLE, BUNDLE, 128, X1, X1, X2, X2)
-P_B, P_OP, P_OM, P_O2, P_XP, P_XM, P_X2P, P_X2M, POOL = (sum(SIZES[:n]) for n in range(len(SIZES) + 1))
+SIZES = (BUNDLE, BUNDLE, BUNDLE, 128, X1, X1, X2, X2, SPEEDS, SPEEDS, SPEEDS)
+P_B, P_OP, P_OM, P_O2, P_XP, P_XM, P_X2P, P_X2M, P_V, P_VP, P_VM, POOL = (
+    sum(SIZES[:n]) for n in range(len(SIZES) + 1)
+)
 
 
 def column_rows():
     out = {(0, 0): P_B, (0, 1): P_OP, (0, -1): P_OM}
     for dx, x1, x2 in ((1, P_XP, P_X2P), (-1, P_XM, P_X2M)):
-        out[dx, 0], out[dx, 1], out[dx, -1] = x1, x1 + BUNDLE, x1 + BUNDLE + AT_V
+        out[dx, 0], out[dx, 1], out[dx, -1] = x1, x1 + BUNDLE, x1 + 2 * BUNDLE
         for n, dy in enumerate((0, 1, -1)):
             out[2 * dx, dy] = x2 + n * 128
     stay = {c: at + AT_S for c, at in out.items() if abs(c[0]) < 2}
     for dy in (-2, 2):
         out[0, dy] = P_O2
         for dx, x1 in ((1, P_XP), (-1, P_XM)):
-            out[dx, dy] = x1 + BUNDLE + 2 * AT_V
+            out[dx, dy] = x1 + 3 * BUNDLE
     return out, stay
 
 
@@ -88,7 +91,7 @@
 
 
 def pack_kernel(*refs):
-    sources, (bundle, alone), held, sems = refs[:8], refs[8:10], refs[10:18], refs[18]
+    sources, (bundle, alone, speeds), held, sems = refs[:8], refs[8:11], refs[11:19], refs[19]
     copies = [pltpu.make_async_copy(a, b, sems.at[n]) for n, (a, b) in enumerate(zip(sources, held))]
     for copy in copies:
         copy.start()
@@ -123,7 +126,7 @@
         one = vel[pl.ds(2 * c, CELLS, stride=6), :]
         two = vel[pl.ds(2 * c + 1, CELLS, stride=6), :]
         speed = jnp.where(filled, jnp.where(low_slot, one, two), 0.0)
-        bundle[pl.ds(AT_V + c, CELLS, stride=3), :] = speed
+        speeds[pl.ds(c, CELLS, stride=3), :] = speed
 
 
 def place():
@@ -143,7 +146,7 @@
     return lax.broadcasted_iota(i32, shape, axis)
 
 
-def edges_kernel(b, op, om, o2, xp, xm, x2p, x2m, low, high):
+def edges_kernel(b, op, om, o2, xp, xm, x2p, x2m, speeds, low, high):
     parts = (
         (P_B, b), (P_OP, op), (P_OM, om), (P_O2, o2),
         (P_XP, xp), (P_XM, xm), (P_X2P, x2p), (P_X2M, x2m),
@@ -173,8 +176,8 @@
             to = EDGE_AT[column] + 8
             ref[to : to + 8, :] = source[row + 4 * cell : row + 4 * cell + 8, :]
         ref[E_T : E_T + 16, :] = table
-        at = AT_V + (88 if side else 0)
-        ref[E_V : E_V + 8, :] = b[at : at + 8, :]
+        at = 88 if side else 0
+        ref[E_V : E_V + 8, :] = speeds[at : at + 8, :]
 
 
 def find_tasks(dest, near_tables, edges, masks, words, heads, occ, turn):
@@ -398,12 +401,13 @@
                 value = vel[pl.ds(2 * (r - 3) + s, CELLS, stride=6), :]
             ext[pl.ds(8 * r + s, CELLS, stride=56), :] = jnp.where(keep, value, 0.0)
     places = (P_XM, P_XP, P_OM, P_OP, P_B, P_B)
+    speeds = (P_XM + X1 - SPEEDS, P_XP + X1 - SPEEDS, P_VM, P_VP, P_V, P_V)
     for f in range(6):
         flag = jnp.broadcast_to(full[2 : 2 + CELLS, f : f + 1], (CELLS, LANES))
         for r in range(7):
             shift = float(FACES[f][r]) if r < 3 else 0.0
             if 3 <= r < 6:
-                at, step = places[f] + AT_V + r - 3, 3
+                at, step = speeds[f] + r - 3, 3
             else:
                 at, step = places[f] + min(r, 3), 4
             inner = CELLS - 1
@@ -619,6 +623,22 @@
 ]
 
 
+def copy_kernel(source, _, result):
+    result[...] = source[...]
+
+
+def held_back(array, other):
+    return pl.pallas_call(
+        copy_kernel,
+        out_shape=rows_of(array.shape[0]),
+        in_specs=[whole()] * 2,
+        out_specs=whole(),
+        cost_estimate=pl.CostEstimate(flops=20 * 10**9, bytes_accessed=2**20, transcendentals=0),
+        compiler_params=limit(8),
+        name="held",
+    )(array, other[:8])
+
+
 def per_device(
     positions,
     velocities,
@@ -634,11 +654,11 @@
     vel = velocities.reshape((CELLS * 6, ATOMS))
     stren = strength.reshape((CELLS * 2, ATOMS))
     dest = destination.reshape((NX * NY, LANES))
-    B, O = pl.pallas_call(
+    B, O, V = pl.pallas_call(
         pack_kernel,
-        out_shape=[rows_of(BUNDLE), rows_of(128)],
+        out_shape=[rows_of(BUNDLE), rows_of(128), rows_of(SPEEDS)],
         in_specs=[whole(pltpu.HBM)] * 8,
-        out_specs=[whole()] * 2,
+        out_specs=[whole()] * 3,
         scratch_shapes=[
             VMEM((CELLS * 6, ATOMS), f32),
             VMEM((CELLS * 2, ATOMS), f32),
@@ -663,20 +683,24 @@
     )
     cat = jnp.concatenate
     O_2 = moved_by(O, "gy", 2)
-    B_p, B_m = moved_by(B, "gy", -1), moved_by(B, "gy", 1)
-    near = cat([B, B_p[:AT_V], B_m[:AT_V], O_2], axis=0)
+    BV_p, B_m = moved_by(cat([B, V], axis=0), "gy", -1), moved_by(B, "gy", 1)
+    B_p, V_p = BV_p[:BUNDLE], BV_p[BUNDLE:]
+    near = cat([B, B_p, B_m, O_2, V], axis=0)
     far = cat([O, B_p[:128], B_m[:128]], axis=0)
     X_p, X_m = moved_by(near, "gx", -1), moved_by(near, "gx", 1)
     X2_p, X2_m = moved_by(far, "gx", -2), moved_by(far, "gx", 2)
+    V_m = moved_by(held_back(V, B_p[:8] + B_m[:8] + O_2[:8]), "gy", 1)
+    V_m = held_back(V_m, V_m)
+    V_e = lax.optimization_barrier((V, V_m))[0]
     buffers = (B, B_p, B_m, O_2, X_p, X_m, X2_p, X2_m)
     low, high = pl.pallas_call(
         edges_kernel,
         out_shape=[rows_of(EDGE), rows_of(EDGE)],
-        in_specs=[whole()] * 8,
+        in_specs=[whole()] * 9,
         out_specs=[whole()] * 2,
         compiler_params=limit(8),
         name="edges",
-    )(*buffers)
+    )(*buffers, V_e)
     zlo, zhi = moved_by(high, "gz", 1), moved_by(low, "gz", -1)
     masks, words = pl.pallas_call(
         flags_kernel,
@@ -687,7 +711,7 @@
         compiler_params=limit(8),
         name="flags",
     )(dest, B, B_p, B_m, X_p, X_m)
-    pool = cat(buffers, axis=0)
+    pool = cat(buffers + (V, V_p, V_m), axis=0)
     ext, early = pl.pallas_call(
         early_kernel,
         out_shape=[rows_of(CELLS * 56), rows_of(CELLS * 24)],

time: 50.8 us -> 47.8 us (0.941)
  waiting for transfers between devices: 17.4 us -> 15 us
  Pallas kernels: 8.56 us -> 7.84 us
    ppermute x9 -> x10, waiting for transfers between devices: 17.4 us -> 15 us  [moved_by(): lax.ppermute(array, axis, [(i, (i + by) % size) for i in range(size)])]
    pallas_call x1, Pallas kernels: 3.69 us -> 2.98 us  [per_device(): pl.pallas_call(early_kernel, out_shape=[rows_of(CELLS * 56), rows_of(CELL...]
    ppermute x9 -> x10, starting transfers between devices: 24 us -> 23.9 us  [moved_by(): lax.ppermute(array, axis, [(i, (i + by) % size) for i in range(size)])]
    pallas_call x1 -> x3, Pallas kernels: 1.31 us -> 1.32 us  [the longest x1 1.31 us: per_device(): pl.pallas_call(pack_kernel, out_shape=[rows_of(BUNDLE), rows_of(128), row...]
  transfers between devices with their start and end apart: 9 -> 10, of which waited for: 5 -> 7; matrix products, arithmetic and copies ran while one was open for 0% -> 0% of each run, Pallas kernels for 8% -> 7%
where the time goes in v3:
time: 47.8 us; the launch traced here: 47.9 us
  starting transfers between devices  23.9 us (50%)
  waiting for transfers between devices  15 us (31%)
  Pallas kernels  7.84 us (16%)
  between operations  0.79 us (2%)
    ppermute x10, starting transfers between devices, moved_by(): lax.ppermute(array, axis, [(i, (i + by) % size) for i in range(size)])  23.9 us
    ppermute x10, waiting for transfers between devices, moved_by(): lax.ppermute(array, axis, [(i, (i + by) % size) for i in range(size)])  15 us
    pallas_call x1, Pallas kernels, per_device(): pl.pallas_call(late_kernel, out_shape=[jax.ShapeDtypeStruct((1, 1, CELLS,...  3.07 us
    pallas_call x1, Pallas kernels, per_device(): pl.pallas_call(early_kernel, out_shape=[rows_of(CELLS * 56), rows_of(CELL...  2.98 us
    pallas_call x1, Pallas kernels, per_device(): pl.pallas_call(pack_kernel, out_shape=[rows_of(BUNDLE), rows_of(128), row...  1.31 us
  transfers between devices with their start and end apart: 10, of which 7 were waited for; matrix products, arithmetic and copies ran while one was open for 0% of the time, Pallas kernels for 7%

profile of v3, /device:TPU:1, one launch (start us, length us, event | category | flops | bytes accessed | tf_op | source)
XLA Modules:
  0.0 47.9 jit_solution(2740266981608223470)
XLA Ops:
  0.6 1.3 %pack.1 = (f32[272,128]{1,0:T(8,128)S(1)}, f32[128,128]{1,0:T(8,128)S(1)}, f32[96,128]{1,0:T(8,128)S(1)}) custom-call(f32[192,128]{1,0:T(8,128)} %bitcast.18, f32[64,128]{1,0:T(8,128)} %bitcast.19, f32[192,128]{1,0:T(8,128)} %bitcast.13, s32[16,32]{1,0:T(8,128)} %bitcast.20, s32[16,32]{1,0:T(8,128)} %bitcast.21, s32[1,32]{1,0:T(1,128)} %bitcast.22, ...), custom_call_target="tpu_custom_call" | custom-call | tf_op jit(solution)/shard_map/pack/pallas_call | solution.py:657
  2.0 6.9 %collective-permute-start = (f32[368,128]{1,0:T(8,128)S(1)}, f32[368,128]{1,0:T(8,128)S(1)}, u32[]{:S(2)}, u32[]{:S(2)}) collective-permute-start(f32[368,128]{1,0:T(8,128)S(1)} %pad_maximum_fusion.1), channel_id=1, source_target_pairs={{0,12},{4,0},{8,4},{12,8},{1,13},{5,1},{9,5},{13,9},{2,14},{6,2},{... | collective-permute-start | bytes 565256 | tf_op jit(solution)/shard_map/ppermute | solution.py:85
  8.9 3.3 %collective-permute-start.2 = (f32[128,128]{1,0:T(8,128)S(1)}, f32[128,128]{1,0:T(8,128)S(1)}, u32[]{:S(2)}, u32[]{:S(2)}) collective-permute-start(f32[128,128]{1,0:T(8,128)S(1)} %get-tuple-element.14), channel_id=1, source_target_pairs={{0,8},{4,12},{8,0},{12,4},{1,9},{5,13},{9,1},{13,5},{2,10},{6,14},... | collective-permute-start | bytes 196616 | tf_op jit(solution)/shard_map/ppermute | solution.py:85
  12.2 4.4 %collective-permute-done.1.om = f32[272,128]{1,0:T(8,128)S(1)} collective-permute-done((f32[272,128]{1,0:T(8,128)S(1)}, f32[272,128]{1,0:T(8,128)S(1)}, u32[]{:S(2)}, u32[]{:S(2)}) %collective-permute-start.1) | collective-permute-done | bytes 139296 | tf_op jit(solution)/shard_map/ppermute | solution.py:85
  16.6 0.0 collective-permute-done
  16.7 0.6 %collective-permute-done.2.o2 = f32[128,128]{1,0:T(8,128)S(1)} collective-permute-done((f32[128,128]{1,0:T(8,128)S(1)}, f32[128,128]{1,0:T(8,128)S(1)}, u32[]{:S(2)}, u32[]{:S(2)}) %collective-permute-start.2) | collective-permute-done | bytes 65568 | tf_op jit(solution)/shard_map/ppermute | solution.py:85
  17.2 4.6 %collective-permute-start.3 = (f32[1040,128]{1,0:T(8,128)S(1)}, f32[1040,128]{1,0:T(8,128)S(1)}, u32[]{:S(2)}, u32[]{:S(2)}) collective-permute-start(f32[1040,128]{1,0:T(8,128)S(1)} %constant_dynamic-update-slice_fusion), channel_id=1, source_target_pairs={{0,240},{16,0},{32,16},{48,32},{64,48},{80,64},{96,80},{112,96},{1... | collective-permute-start | bytes 1597448 | tf_op jit(solution)/shard_map/ppermute | solution.py:85
  21.8 1.3 %collective-permute-start.4 = (f32[1040,128]{1,0:T(8,128)S(1)}, f32[1040,128]{1,0:T(8,128)S(1)}, u32[]{:S(2)}, u32[]{:S(2)}) collective-permute-start(f32[1040,128]{1,0:T(8,128)S(1)} %constant_dynamic-update-slice_fusion), channel_id=1, source_target_pairs={{0,16},{16,32},{32,48},{48,64},{64,80},{80,96},{96,112},{112,128},... | collective-permute-start | bytes 1597448 | tf_op jit(solution)/shard_map/ppermute | solution.py:85
  23.1 2.8 %collective-permute-start.7 = (f32[96,128]{1,0:T(8,128)S(1)}, f32[96,128]{1,0:T(8,128)S(1)}, u32[]{:S(2)}, u32[]{:S(2)}) collective-permute-start(f32[96,128]{1,0:T(8,128)S(1)} %held.2), channel_id=1, source_target_pairs={{0,4},{4,8},{8,12},{12,0},{1,5},{5,9},{9,13},{13,1},{2,6},{6,10},{... | collective-permute-start | bytes 147464 | tf_op jit(solution)/shard_map/ppermute | solution.py:85
  25.9 2.4 %collective-permute-start.5 = (f32[384,128]{1,0:T(8,128)S(1)}, f32[384,128]{1,0:T(8,128)S(1)}, u32[]{:S(2)}, u32[]{:S(2)}) collective-permute-start(f32[384,128]{1,0:T(8,128)S(1)} %pad_maximum_fusion), channel_id=1, source_target_pairs={{0,224},{16,240},{32,0},{48,16},{64,32},{80,48},{96,64},{112,80},{... | collective-permute-start | bytes 589832 | tf_op jit(solution)/shard_map/ppermute | solution.py:85
  28.3 0.0 collective-permute-start.6
  28.3 1.3 %collective-permute-done.7.source = f32[96,128]{1,0:T(8,128)S(1)} collective-permute-done((f32[96,128]{1,0:T(8,128)S(1)}, f32[96,128]{1,0:T(8,128)S(1)}, u32[]{:S(2)}, u32[]{:S(2)}) %collective-permute-start.7) | collective-permute-done | bytes 49184 | tf_op jit(solution)/shard_map/ppermute | solution.py:85
  29.6 2.2 %collective-permute-done.3.xp = f32[1040,128]{1,0:T(8,128)S(1)} collective-permute-done((f32[1040,128]{1,0:T(8,128)S(1)}, f32[1040,128]{1,0:T(8,128)S(1)}, u32[]{:S(2)}, u32[]{:S(2)}) %collective-permute-start.3) | collective-permute-done | bytes 532512 | tf_op jit(solution)/shard_map/ppermute | solution.py:85
  31.8 0.0 copy-start.1
  31.9 1.7 %collective-permute-done.5.x2p = f32[384,128]{1,0:T(8,128)S(1)} collective-permute-done((f32[384,128]{1,0:T(8,128)S(1)}, f32[384,128]{1,0:T(8,128)S(1)}, u32[]{:S(2)}, u32[]{:S(2)}) %collective-permute-start.5) | collective-permute-done | bytes 196640 | tf_op jit(solution)/shard_map/ppermute | solution.py:85
  33.6 0.0 copy-start
  33.6 4.8 %collective-permute-done.6.x2m = f32[384,128]{1,0:T(8,128)S(1)} collective-permute-done((f32[384,128]{1,0:T(8,128)S(1)}, f32[384,128]{1,0:T(8,128)S(1)}, u32[]{:S(2)}, u32[]{:S(2)}) %collective-permute-start.6) | collective-permute-done | bytes 196640 | tf_op jit(solution)/shard_map/ppermute | solution.py:85
  38.4 0.1 edges.1
  38.5 1.3 %collective-permute-start.8 = (f32[240,128]{1,0:T(8,128)S(1)}, f32[240,128]{1,0:T(8,128)S(1)}, u32[]{:S(2)}, u32[]{:S(2)}) collective-permute-start(f32[240,128]{1,0:T(8,128)S(1)} %get-tuple-element.16), channel_id=1, source_target_pairs={{0,1},{1,2},{2,3},{3,0},{4,5},{5,6},{6,7},{7,4},{8,9},{9,10},{10,1... | collective-permute-start | bytes 368648 | tf_op jit(solution)/shard_map/ppermute | solution.py:85
  39.8 1.5 %collective-permute-start.9 = (f32[240,128]{1,0:T(8,128)S(1)}, f32[240,128]{1,0:T(8,128)S(1)}, u32[]{:S(2)}, u32[]{:S(2)}) collective-permute-start(f32[240,128]{1,0:T(8,128)S(1)} %get-tuple-element.17), channel_id=1, source_target_pairs={{0,3},{1,0},{2,1},{3,2},{4,7},{5,4},{6,5},{7,6},{8,11},{9,8},{10,9... | collective-permute-start | bytes 368648 | tf_op jit(solution)/shard_map/ppermute | solution.py:85
  41.3 0.4 flags.1
  41.7 3.0 %early.1 = (f32[1792,128]{1,0:T(8,128)S(1)}, f32[768,128]{1,0:T(8,128)S(1)}) custom-call(s32[64,128]{1,0:T(8,128)S(1)} %bitcast.16, f32[192,128]{1,0:T(8,128)S(1)} %bitcast.14, f32[4080,128]{1,0:T(8,128)S(1)} %constant_dynamic-update-slice_fusion.5.pool, s32[8,128]{1,0:T(8,128)S(1)} %get-tuple-element.18.masks.done, s32[32,128]{1,0:T(8,128)S(1)} %get-tuple-element.19.words), custom_call_target="tpu_custom_call" | custom-call | tf_op jit(solution)/shard_map/early/pallas_call | solution.py:715
  44.6 0.1 collective-permute-done.8.zlo
  44.8 3.1 %late.1 = (f32[1,1,32,6,8,128]{5,4,3,2,1,0:T(8,128)}, f32[1,1,32,3,8,128]{5,4,3,2,1,0:T(8,128)}) custom-call(s32[64,128]{1,0:T(8,128)S(1)} %bitcast.17, f32[4080,128]{1,0:T(8,128)S(1)} %constant_dynamic-update-slice_fusion.5.pool, f32[240,128]{1,0:T(8,128)S(1)} %collective-permute-done.8.zlo, f32[240,128]{1,0:T(8,128)S(1)} %collective-permute-done.9.zhi, ...), custom_call_target="tpu_custom_call" | custom-call | tf_op jit(solution)/shard_map/late/pallas_call | solution.py:724
  (25 shorter events, 0.3 us)
Async XLA Ops:
  2.0 14.6 %collective-permute-start = (f32[368,128]{1,0:T(8,128)S(1)}, f32[368,128]{1,0:T(8,128)S(1)}, u32[]{:S(2)}, u32[]{:S(2)}) collective-permute-start(f32[368,128]{1,0:T(8,128)S(1)} %pad_maximum_fusion.1), channel_id=1, source_target_pairs={{0,12},{4,0},{8,4},{12,8},{1,13},{5,1},{9,5},{13,9},{2,14},{6,2},{... | collective-permute-start | bytes 565256 | tf_op jit(solution)/shard_map/ppermute | solution.py:85
  8.9 7.7 %collective-permute-start.1 = (f32[272,128]{1,0:T(8,128)S(1)}, f32[272,128]{1,0:T(8,128)S(1)}, u32[]{:S(2)}, u32[]{:S(2)}) collective-permute-start(f32[272,128]{1,0:T(8,128)S(1)} %get-tuple-element.12.b), channel_id=1, source_target_pairs={{0,4},{4,8},{8,12},{12,0},{1,5},{5,9},{9,13},{13,1},{2,6},{6,10},{... | collective-permute-start | bytes 417800 | tf_op jit(solution)/shard_map/ppermute | solution.py:85
  8.9 8.3 %collective-permute-start.2 = (f32[128,128]{1,0:T(8,128)S(1)}, f32[128,128]{1,0:T(8,128)S(1)}, u32[]{:S(2)}, u32[]{:S(2)}) collective-permute-start(f32[128,128]{1,0:T(8,128)S(1)} %get-tuple-element.14), channel_id=1, source_target_pairs={{0,8},{4,12},{8,0},{12,4},{1,9},{5,13},{9,1},{13,5},{2,10},{6,14},... | collective-permute-start | bytes 196616 | tf_op jit(solution)/shard_map/ppermute | solution.py:85
  17.2 14.5 %collective-permute-start.3 = (f32[1040,128]{1,0:T(8,128)S(1)}, f32[1040,128]{1,0:T(8,128)S(1)}, u32[]{:S(2)}, u32[]{:S(2)}) collective-permute-start(f32[1040,128]{1,0:T(8,128)S(1)} %constant_dynamic-update-slice_fusion), channel_id=1, source_target_pairs={{0,240},{16,0},{32,16},{48,32},{64,48},{80,64},{96,80},{112,96},{1... | collective-permute-start | bytes 1597448 | tf_op jit(solution)/shard_map/ppermute | solution.py:85
  21.8 10.0 %collective-permute-start.4 = (f32[1040,128]{1,0:T(8,128)S(1)}, f32[1040,128]{1,0:T(8,128)S(1)}, u32[]{:S(2)}, u32[]{:S(2)}) collective-permute-start(f32[1040,128]{1,0:T(8,128)S(1)} %constant_dynamic-update-slice_fusion), channel_id=1, source_target_pairs={{0,16},{16,32},{32,48},{48,64},{64,80},{80,96},{96,112},{112,128},... | collective-permute-start | bytes 1597448 | tf_op jit(solution)/shard_map/ppermute | solution.py:85
  23.1 6.5 %collective-permute-start.7 = (f32[96,128]{1,0:T(8,128)S(1)}, f32[96,128]{1,0:T(8,128)S(1)}, u32[]{:S(2)}, u32[]{:S(2)}) collective-permute-start(f32[96,128]{1,0:T(8,128)S(1)} %held.2), channel_id=1, source_target_pairs={{0,4},{4,8},{8,12},{12,0},{1,5},{5,9},{9,13},{13,1},{2,6},{6,10},{... | collective-permute-start | bytes 147464 | tf_op jit(solution)/shard_map/ppermute | solution.py:85
  25.9 7.6 %collective-permute-start.5 = (f32[384,128]{1,0:T(8,128)S(1)}, f32[384,128]{1,0:T(8,128)S(1)}, u32[]{:S(2)}, u32[]{:S(2)}) collective-permute-start(f32[384,128]{1,0:T(8,128)S(1)} %pad_maximum_fusion), channel_id=1, source_target_pairs={{0,224},{16,240},{32,0},{48,16},{64,32},{80,48},{96,64},{112,80},{... | collective-permute-start | bytes 589832 | tf_op jit(solution)/shard_map/ppermute | solution.py:85
  28.3 10.1 %collective-permute-start.6 = (f32[384,128]{1,0:T(8,128)S(1)}, f32[384,128]{1,0:T(8,128)S(1)}, u32[]{:S(2)}, u32[]{:S(2)}) collective-permute-start(f32[384,128]{1,0:T(8,128)S(1)} %pad_maximum_fusion), channel_id=1, source_target_pairs={{0,32},{16,48},{32,64},{48,80},{64,96},{80,112},{96,128},{112,144}... | collective-permute-start | bytes 589832 | tf_op jit(solution)/shard_map/ppermute | solution.py:85
  31.8 9.5 %copy-start.1 = (s32[16,4,128]{2,1,0:T(4,128)S(1)}, s32[16,4,128]{2,1,0:T(4,128)}, u32[]{:S(2)}) copy-start(s32[16,4,128]{2,1,0:T(4,128)} %param.14) | copy-start | bytes 98308
  33.6 8.1 %copy-start = (f32[1,1,32,3,2,128]{5,4,3,2,1,0:T(2,128)S(1)}, f32[1,1,32,3,2,128]{5,4,3,2,1,0:T(2,128)}, u32[]{:S(2)}) copy-start(f32[1,1,32,3,2,128]{5,4,3,2,1,0:T(2,128)} %param.10) | copy-start | bytes 294916
  38.5 6.3 %collective-permute-start.8 = (f32[240,128]{1,0:T(8,128)S(1)}, f32[240,128]{1,0:T(8,128)S(1)}, u32[]{:S(2)}, u32[]{:S(2)}) collective-permute-start(f32[240,128]{1,0:T(8,128)S(1)} %get-tuple-element.16), channel_id=1, source_target_pairs={{0,1},{1,2},{2,3},{3,0},{4,5},{5,6},{6,7},{7,4},{8,9},{9,10},{10,1... | collective-permute-start | bytes 368648 | tf_op jit(solution)/shard_map/ppermute | solution.py:85
  39.8 5.0 %collective-permute-start.9 = (f32[240,128]{1,0:T(8,128)S(1)}, f32[240,128]{1,0:T(8,128)S(1)}, u32[]{:S(2)}, u32[]{:S(2)}) collective-permute-start(f32[240,128]{1,0:T(8,128)S(1)} %get-tuple-element.17), channel_id=1, source_target_pairs={{0,3},{1,0},{2,1},{3,2},{4,7},{5,4},{6,5},{7,6},{8,11},{9,8},{10,9... | collective-permute-start | bytes 368648 | tf_op jit(solution)/shard_map/ppermute | solution.py:85
